TPU v7x, 32 devices: a whole 2x2x4 slice. The times are simulated.
32 devices in a mesh: comp: 16 (over z, x, core), space: 2 (over y).
Axes of the slice: x: 2, y: 2, z: 4, core: 2. Of those that a mesh axis runs over, the one named last changes fastest.
Arguments:
- spectrum: float32 [1152, 16384], P(None, ('comp', 'space')), may hold values from 0.05 to 1
- wind_field: float32 [2, 16384], P(None, ('comp', 'space')), may hold values from -4 to 4
- coupling: bfloat16 [1152, 1152], replicated, may hold values from -0.1875 to 0.1875
- growth: float32 [32], replicated, may hold values from 0.02 to 0.2
- dissipation: float32 [32], replicated, may hold values from 0.1 to 1
- group_speed: float32 [32, 32], replicated, may hold values from 0.1 to 0.45
- refraction: float32 [32, 32], replicated, may hold values from -0.5 to 0.5
- depths: float32 [32], replicated, may hold values from 0.1 to 1
- sea_mask: int32 [128, 128], P('space'), may hold values 0 or 1
- depth_index: int32 [128, 128], P('space'), may hold values from 0 to 31
Outputs:
- spectrum_out: float32 [1152, 16384], P(None, ('comp', 'space'))
All inputs are finite; a program needn't handle non-finite values. No bound on the sum of `sea_mask` on one device may be relied on, other than what follows from the above.
Results may differ from a plain program's by a relative error of at most 0.00051.
Values sent between devices are 32-bit elements; how exact they have to be, the bound alone decides.
No kernel may reach another device: no remote copies, remote signals or barrier semaphores. Data moves between devices by JAX's collectives and lax.ppermute only.
A program may use at most 64 MiB of HBM per device.

v0:
```python
import jax
import jax.numpy as jnp
from jax import lax
from jax.sharding import PartitionSpec as P

ND = 36
SUBSTEPS = 3


def extended(shard, sides, width):
    for axis, dim in sides:
        size, length = (lax.axis_size(axis), shard.shape[dim])
        up = [(i, (i + 1) % size) for i in range(size - 1)]
        down = [(j, i) for i, j in up]
        last = lax.slice_in_dim(shard, length - width, length, axis=dim)
        leading = lax.slice_in_dim(shard, 0, width, axis=dim)
        before = lax.ppermute(last, axis, up)
        after = lax.ppermute(leading, axis, down)
        shard = jnp.concatenate([before, shard, after], axis=dim)
    return shard


def direction_angles():
    return 2.0 * jnp.pi * jnp.arange(ND, dtype=jnp.float32) / ND


def source_terms(energy, wind_block, coupling, growth, dissipation):
    nfreq = growth.shape[0]
    angles = direction_angles()
    projected = (
        jnp.cos(angles)[:, None] * wind_block[0][None, :]
        + jnp.sin(angles)[:, None] * wind_block[1][None, :]
    )
    forcing = jnp.maximum(projected, 0.0)
    driving = growth[:, None, None] * (forcing * forcing)[None]
    average = jnp.mean(energy, axis=0)
    damping = dissipation[:, None, None] * (average / (average + 1.0))[None, None, :]
    nonlinear = jnp.dot(coupling, energy.astype(jnp.bfloat16), preferred_element_type=jnp.float32)
    shaped = energy.reshape(nfreq, ND, -1)
    return (shaped + (driving - damping) * shaped).reshape(energy.shape) + 0.25 * nonlinear


def face_flux(behind, centre, forward, beyond, courant):
    central = 0.5 * (centre + forward) - 0.5 * courant * (forward - centre)
    curvature = jnp.where(
        courant >= 0.0, forward - 2.0 * centre + behind, beyond - 2.0 * forward + centre
    )
    return courant * (central - (1.0 - courant * courant) / 6.0 * curvature)


def cut_along(values, offset, length, along):
    return lax.slice_in_dim(values, offset, offset + length, axis=along)


def advect(padded, speeds, weight, along):
    inner_count = padded.shape[along] - 4
    courant = 0.5 * (
        cut_along(speeds, 1, inner_count + 1, along) + cut_along(speeds, 2, inner_count + 1, along)
    )
    if weight is not None:
        courant = (
            courant
            * cut_along(weight, 1, inner_count + 1, along)
            * cut_along(weight, 2, inner_count + 1, along)
        )
    face_values = face_flux(
        cut_along(padded, 0, inner_count + 1, along),
        cut_along(padded, 1, inner_count + 1, along),
        cut_along(padded, 2, inner_count + 1, along),
        cut_along(padded, 3, inner_count + 1, along),
        courant,
    )
    return cut_along(padded, 2, inner_count, along) - (
        cut_along(face_values, 1, inner_count, along)
        - cut_along(face_values, 0, inner_count, along)
    )


def pad_zero(values, along, width):
    padding = [(0, 0)] * values.ndim
    padding[along] = (width, width)
    return jnp.pad(values, padding)


def wrap_dirs(values, along):
    length = values.shape[along]
    return jnp.concatenate(
        [cut_along(values, length - 2, 2, along), values, cut_along(values, 0, 2, along)],
        axis=along,
    )


def surface_slopes(height):
    rows_padded = jnp.pad(height, ((1, 1), (0, 0)))
    cols_padded = jnp.pad(height, ((0, 0), (1, 1)))
    return (
        0.5 * (rows_padded[2:] - rows_padded[:-2]),
        0.5 * (cols_padded[:, 2:] - cols_padded[:, :-2]),
    )


def transport_speeds(speed_pts, refract_pts, height):
    angles = direction_angles()
    cosine_dir = jnp.cos(angles)[:, None, None]
    sine_dir = jnp.sin(angles)[:, None, None]
    slope_x, slope_y = surface_slopes(height)
    speed_wide = jnp.expand_dims(speed_pts, -3)
    speed_x = speed_wide * cosine_dir
    speed_y = speed_wide * sine_dir
    speed_dir = jnp.expand_dims(refract_pts, -3) * (sine_dir * slope_x - cosine_dir * slope_y)
    return (speed_x, speed_y, speed_dir)


def cross_passes(energy, speed_y, speed_dir, mask_wide):
    y_axis = energy.ndim - 1
    dir_axis = energy.ndim - 3
    energy = advect(
        pad_zero(energy, y_axis, 2),
        pad_zero(speed_y, y_axis, 2),
        pad_zero(mask_wide, y_axis, 2),
        y_axis,
    )
    energy = advect(wrap_dirs(energy, dir_axis), wrap_dirs(speed_dir, dir_axis), None, dir_axis)
    return energy * mask_wide


def per_device(
    spectrum,
    wind_field,
    coupling,
    growth,
    dissipation,
    group_speed,
    refraction,
    depths,
    sea_mask,
    depth_index,
):
    comp_count = lax.axis_size("comp")
    components = spectrum.shape[0]
    group_size = components // comp_count
    nfreq_local = group_size // ND
    strip_rows = sea_mask.shape[0]
    width_y = sea_mask.shape[1]
    regrouped = lax.all_to_all(
        source_terms(spectrum, wind_field, coupling, growth, dissipation),
        "comp",
        split_axis=0,
        concat_axis=1,
        tiled=True,
    )
    energy = regrouped.reshape(nfreq_local, ND, strip_rows, width_y)
    margin = 2
    coast_cells = extended(jnp.stack([sea_mask, depth_index]), (("space", 1),), margin)
    mask_ext = coast_cells[0].astype(jnp.float32)
    levels = depths.shape[0]
    onehot = (coast_cells[1].reshape(1, -1) == jnp.arange(levels, dtype=jnp.int32)[:, None]).astype(
        jnp.float32
    )
    first_freq = lax.axis_index("comp") * nfreq_local
    tables = jnp.concatenate(
        [
            depths[None, :],
            lax.dynamic_slice_in_dim(group_speed, first_freq, nfreq_local, 0),
            lax.dynamic_slice_in_dim(refraction, first_freq, nfreq_local, 0),
        ],
        axis=0,
    )
    looked = jnp.dot(tables, onehot, precision=lax.Precision.HIGHEST).reshape(
        1 + 2 * nfreq_local, strip_rows + 2 * margin, width_y
    )
    height = looked[0] * mask_ext
    speed_x, speed_y, speed_dir = transport_speeds(
        looked[1 : 1 + nfreq_local], looked[1 + nfreq_local :], height
    )
    mask_wide = mask_ext[None, None]
    for substep in range(SUBSTEPS):
        padded = extended(energy, (("space", 2),), 2)
        energy = advect(padded, speed_x, mask_wide, 2)
        energy = cross_passes(
            energy, speed_y[:, :, 2:-2], speed_dir[:, :, 2:-2], mask_wide[:, :, 2:-2]
        )
    flattened = energy.reshape(group_size, strip_rows * width_y)
    return lax.all_to_all(flattened, "comp", split_axis=1, concat_axis=0, tiled=True)


def solution(mesh):
    in_specs = (
        P(None, ("comp", "space")),
        P(None, ("comp", "space")),
        P(),
        P(),
        P(),
        P(),
        P(),
        P(),
        P("space", None),
        P("space", None),
    )
    out_specs = P(None, ("comp", "space"))
    return jax.shard_map(
        per_device, mesh=mesh, in_specs=in_specs, out_specs=out_specs, check_vma=False
    )
```

profile of v0, /device:TPU:1, one launch (start us, length us, event | category | flops | bytes accessed | tf_op | source)
XLA Modules:
  0.0 218.6 jit_solution(14488815422492544405)
XLA Ops:
  0.0 0.9 pad_add_fusion.2
  0.9 4.0 %collective-permute-start = (s32[2,2,128]{2,1,0:T(2,128)S(1)}, s32[2,2,128]{2,1,0:T(2,128)S(1)}, u32[]{:S(2)}, u32[]{:S(2)}) collective-permute-start(s32[2,2,128]{2,1,0:T(2,128)S(1)} %get-tuple-element.27), channel_id=1, source_target_pairs={{0,1},{2,3},{4,5},{6,7},{8,9},{10,11},{12,13},{14,15},{16,17},{18,... | collective-permute-start | bytes 6152 | tf_op jit(solution)/shard_map/ppermute | solution.py:17
  4.9 1.3 collective-permute-start.1
  6.2 0.8 fusion.115
  7.0 0.1 maximum_multiply_fusion
  7.1 1.8 mul.495
  8.9 3.4 %mul.496 = f32[1152,512]{1,0:T(8,128)} reshape(f32[32,36,512]{2,1,0:T(8,128)} %mul.495) | data formatting | bytes 4718592 | tf_op jit(solution)/shard_map/mul | solution.py:35
  12.3 1.9 reduce_sum.9
  14.2 0.1 broadcast_multiply_fusion.3
  14.3 1.8 sub.228
  16.1 3.4 %sub.229 = f32[1152,512]{1,0:T(8,128)} reshape(f32[32,36,512]{2,1,0:T(8,128)} %sub.228) | data formatting | bytes 4718592 | tf_op jit(solution)/shard_map/sub | solution.py:40
  19.5 0.1 mul.485
  19.6 0.1 mul.486
  19.7 7.0 %fusion.24 = f32[1152,512]{1,0:T(8,128)} fusion(bf16[1152,1152]{1,0:T(8,128)(2,1)S(1)} %copy-done, f32[1152,512]{1,0:T(8,128)} %param.10, f32[1152,512]{1,0:T(8,128)} %sub.229, f32[1152,512]{1,0:T(8,128)} %mul.496, f32[1152]{0:T(1024)S(1)} %mul.486), kind=kOutput, calls=%fused_computation.41 | convolution fusion | flops 1363083264 | bytes 12096000 | tf_op jit(solution)/shard_map/dot_general | solution.py:38
  26.7 6.9 %all-to-all-start = ((f32[16,72,512]{2,1,0:T(8,128)}), f32[16,72,512]{2,1,0:T(8,128)S(1)}, u32[]{:S(2)}, u32[]{:S(2)}) async-start(f32[16,72,512]{2,1,0:T(8,128)} %bitcast.33), calls=%async_computation | async-start | bytes 4718592 | tf_op jit(solution)/shard_map/all_to_all | solution.py:145
  33.7 0.7 constant_dynamic-slice_fusion
  34.4 0.4 fusion.88
  35.1 0.1 slice_reduce_fusion
  35.2 0.1 subtract_multiply_fusion.3
  35.3 0.2 multiply_subtract_fusion
  35.5 0.2 broadcast_multiply_fusion
  35.7 1.8 slice.468
  37.5 0.1 fusion.91
  37.7 1.6 broadcast_multiply_fusion.2
  39.3 1.7 broadcast_multiply_fusion.1
  41.0 38.7 %all-to-all-done = f32[16,72,512]{2,1,0:T(8,128)S(1)} async-done(((f32[16,72,512]{2,1,0:T(8,128)}), f32[16,72,512]{2,1,0:T(8,128)S(1)}, u32[]{:S(2)}, u32[]{:S(2)}) %all-to-all-start) | async-done | bytes 2359328 | tf_op jit(solution)/shard_map/all_to_all | solution.py:145
  79.7 2.8 %copy.14 = f32[72,16,512]{2,1,0:T(8,128)} copy(f32[72,16,512]{2,0,1:T(8,128)S(1)} %bitcast.31) | data formatting | bytes 4718592 | tf_op jit(solution)/shard_map/all_to_all | solution.py:145
  82.5 2.3 %reshape.168 = f32[2,36,64,128]{3,2,1,0:T(8,128)S(1)} reshape(f32[72,16,512]{2,1,0:T(8,128)} %copy.14) | data formatting | bytes 4718592 | tf_op jit(solution)/shard_map/reshape | solution.py:152
  84.9 1.6 collective-permute-start.3
  86.4 0.2 constant_dynamic-update-slice_fusion.1
  86.6 4.4 %collective-permute-start.2 = (f32[2,36,2,128]{3,2,1,0:T(2,128)S(1)}, f32[2,36,2,128]{3,2,1,0:T(2,128)S(1)}, u32[]{:S(2)}, u32[]{:S(2)}) collective-permute-start(f32[2,36,2,128]{3,2,1,0:T(2,128)S(1)} %get-tuple-element.21), channel_id=1, source_target_pairs={{0,1},{2,3},{4,5},{6,7},{8,9},{10,11},{12,13},{14,15},{16,17},{18,... | collective-permute-start | bytes 221192 | tf_op jit(solution)/shard_map/ppermute | solution.py:17
  91.1 0.3 collective-permute-done.3
  91.5 1.3 collective-permute-done.2
  92.8 2.9 %fusion.43 = (f32[2,36,65,128]{3,2,1,0:T(8,128)S(1)}, f32[2,36,65,128]{3,2,1,0:T(8,128)S(1)}) fusion(f32[2,36,66,128]{3,2,1,0:T(8,128)S(1)} %constant_dynamic-update-slice_fusion, f32[2,36,64,128]{3,2,1,0:T(8,128)S(1)} %reshape.168, f32[2,36,2,128]{3,2,1,0:T(2,128)S(1)} %collective-permute-done.2, f32[65,128]{1,0:T(8,128)S(1)} %get-tuple-element.34, ...), kind=kLoop, calls=%fused_computation.69 | loop fusion | flops 14976000 | bytes 16876544 | tf_op jit(solution)/shard_map/mul | solution.py:48
  95.7 0.6 fusion.86
  96.3 1.1 copy-done.4
  97.4 4.9 %fusion.7 = (f32[2,36,64,129]{3,2,1,0:T(8,128)S(1)}, f32[2,36,64,129]{3,2,1,0:T(8,128)S(1)}) fusion(f32[2,36,64,128]{3,2,1,0:T(8,128)S(1)} %fusion.86, f32[64,129]{1,0:T(8,128)S(1)} %get-tuple-element.36, f32[64,129]{1,0:T(8,128)S(1)} %get-tuple-element.35, f32[2,36,64,128]{3,2,1,0:T(8,128)S(1)} %copy-done.4), kind=kLoop, calls=%fused_computation.21 | loop fusion | flops 13671936 | bytes 9540096 | tf_op jit(solution)/shard_map/mul | solution.py:48
  102.3 0.8 fusion.85
  103.1 0.9 copy-done.2
  103.9 2.0 fusion.72
  106.0 0.5 fusion.84
  106.6 4.1 %collective-permute-start.4 = (f32[2,36,2,128]{3,2,1,0:T(2,128)S(1)}, f32[2,36,2,128]{3,2,1,0:T(2,128)S(1)}, u32[]{:S(2)}, u32[]{:S(2)}) collective-permute-start(f32[2,36,2,128]{3,2,1,0:T(2,128)S(1)} %get-tuple-element.17), channel_id=1, source_target_pairs={{0,1},{2,3},{4,5},{6,7},{8,9},{10,11},{12,13},{14,15},{16,17},{18,... | collective-permute-start | bytes 221192 | tf_op jit(solution)/shard_map/ppermute | solution.py:17
  110.7 1.3 collective-permute-start.5
  112.0 0.1 collective-permute-done.4
  112.1 3.7 %collective-permute-done.5 = f32[2,36,2,128]{3,2,1,0:T(2,128)S(1)} collective-permute-done((f32[2,36,2,128]{3,2,1,0:T(2,128)S(1)}, f32[2,36,2,128]{3,2,1,0:T(2,128)S(1)}, u32[]{:S(2)}, u32[]{:S(2)}) %collective-permute-start.5) | collective-permute-done | bytes 73760 | tf_op jit(solution)/shard_map/ppermute | solution.py:18
  115.8 2.5 %fusion.37 = f32[2,36,65,128]{3,2,1,0:T(8,128)S(1)} fusion(f32[2,36,65,128]{3,2,1,0:T(8,128)S(1)} %get-tuple-element.8, f32[2,36,2,128]{3,2,1,0:T(2,128)S(1)} %collective-permute-done.5, f32[2,36,64,128]{3,2,1,0:T(8,128)S(1)} %fusion.84, f32[2,36,2,128]{3,2,1,0:T(2,128)S(1)} %collective-permute-done.4), kind=kLoop, calls=%fused_computation.59 | loop fusion | flops 14376960 | bytes 7299072 | tf_op jit(solution)/shard_map/mul | solution.py:48
  118.3 0.6 fusion.82
  118.9 3.6 %fusion.14 = f32[2,36,64,129]{3,2,1,0:T(8,128)S(1)} fusion(f32[2,36,64,129]{3,2,1,0:T(8,128)S(1)} %get-tuple-element.6, f32[2,36,64,128]{3,2,1,0:T(8,128)S(1)} %fusion.82), kind=kLoop, calls=%fused_computation.28 | loop fusion | flops 11888640 | bytes 7114752 | tf_op jit(solution)/shard_map/mul | solution.py:48
  122.5 0.7 fusion.81
  123.3 2.0 fusion.65
  125.4 0.5 fusion.80
  125.9 1.6 collective-permute-start.6
  127.5 1.5 collective-permute-start.7
  129.1 3.6 %collective-permute-done.7 = f32[2,36,2,128]{3,2,1,0:T(2,128)S(1)} collective-permute-done((f32[2,36,2,128]{3,2,1,0:T(2,128)S(1)}, f32[2,36,2,128]{3,2,1,0:T(2,128)S(1)}, u32[]{:S(2)}, u32[]{:S(2)}) %collective-permute-start.7) | collective-permute-done | bytes 73760 | tf_op jit(solution)/shard_map/ppermute | solution.py:18
  132.6 2.5 %fusion.30 = f32[2,36,65,128]{3,2,1,0:T(8,128)S(1)} fusion(f32[2,36,65,128]{3,2,1,0:T(8,128)S(1)} %get-tuple-element.8, f32[2,36,2,128]{3,2,1,0:T(2,128)S(1)} %collective-permute-done.7, f32[2,36,64,128]{3,2,1,0:T(8,128)S(1)} %fusion.80, f32[2,36,2,128]{3,2,1,0:T(2,128)S(1)} %collective-permute-done.6), kind=kLoop, calls=%fused_computation.48 | loop fusion | flops 14376960 | bytes 7299072 | tf_op jit(solution)/shard_map/mul | solution.py:48
  135.2 0.6 fusion.78
  135.8 3.6 %fusion.21 = f32[2,36,64,129]{3,2,1,0:T(8,128)S(1)} fusion(f32[2,36,64,129]{3,2,1,0:T(8,128)S(1)} %get-tuple-element.6, f32[2,36,64,128]{3,2,1,0:T(8,128)S(1)} %fusion.78), kind=kLoop, calls=%fused_computation.35 | loop fusion | flops 11888640 | bytes 7114752 | tf_op jit(solution)/shard_map/mul | solution.py:48
  139.4 0.7 fusion.77
  140.1 2.0 fusion.58
  142.2 1.9 fusion.76
  144.1 2.4 %all_to_all.29 = f32[72,16,512]{2,1,0:T(8,128)S(1)} reshape(f32[2,36,64,128]{3,2,1,0:T(8,128)} %fusion.76) | data formatting | bytes 4718592 | tf_op jit(solution)/shard_map/all_to_all | solution.py:184
  146.6 1.4 copy.15
  148.0 69.3 %all_to_all.35 = f32[72,16,512]{2,0,1:T(8,128)S(1)} all-to-all(f32[72,16,512]{2,0,1:T(8,128)S(1)} %copy.15), channel_id=1, replica_groups=mesh['comp'=16,'space'=2] {'comp'}, dimensions={1} | all-to-all | bytes 4718592 | tf_op jit(solution)/shard_map/all_to_all | solution.py:184
  217.2 1.4 copy.18
  (40 shorter events, 0.6 us)
Async XLA Ops:
  0.0 19.7 %copy-start = (bf16[1152,1152]{1,0:T(8,128)(2,1)S(1)}, bf16[1152,1152]{1,0:T(8,128)(2,1)}, u32[]{:S(2)}) copy-start(bf16[1152,1152]{1,0:T(8,128)(2,1)} %param.12) | copy-start | bytes 7962628
  0.9 33.5 %collective-permute-start = (s32[2,2,128]{2,1,0:T(2,128)S(1)}, s32[2,2,128]{2,1,0:T(2,128)S(1)}, u32[]{:S(2)}, u32[]{:S(2)}) collective-permute-start(s32[2,2,128]{2,1,0:T(2,128)S(1)} %get-tuple-element.27), channel_id=1, source_target_pairs={{0,1},{2,3},{4,5},{6,7},{8,9},{10,11},{12,13},{14,15},{16,17},{18,... | collective-permute-start | bytes 6152 | tf_op jit(solution)/shard_map/ppermute | solution.py:17
  4.9 29.5 %collective-permute-start.1 = (s32[2,2,128]{2,1,0:T(2,128)S(1)}, s32[2,2,128]{2,1,0:T(2,128)S(1)}, u32[]{:S(2)}, u32[]{:S(2)}) collective-permute-start(s32[2,2,128]{2,1,0:T(2,128)S(1)} %get-tuple-element.28), channel_id=1, source_target_pairs={{1,0},{3,2},{5,4},{7,6},{9,8},{11,10},{13,12},{15,14},{17,16},{19,... | collective-permute-start | bytes 6152 | tf_op jit(solution)/shard_map/ppermute | solution.py:18
  8.9 5.3 %copy-start.7 = (f32[32]{0:T(128)S(1)}, f32[32]{0:T(128)}, u32[]{:S(2)}) copy-start(f32[32]{0:T(128)} %param.14) | copy-start | bytes 388
  16.1 3.4 %copy-start.9 = (f32[32]{0:T(128)S(1)}, f32[32]{0:T(128)}, u32[]{:S(2)}) copy-start(f32[32]{0:T(128)} %param.13) | copy-start | bytes 388
  26.7 7.6 %copy-start.5 = (s32[64,128]{1,0:T(8,128)S(1)}, s32[64,128]{1,0:T(8,128)}, u32[]{:S(2)}) copy-start(s32[64,128]{1,0:T(8,128)} %param.19) | copy-start | bytes 98308
  26.7 7.6 %copy-start.6 = (s32[64,128]{1,0:T(8,128)S(1)}, s32[64,128]{1,0:T(8,128)}, u32[]{:S(2)}) copy-start(s32[64,128]{1,0:T(8,128)} %param.18) | copy-start | bytes 98308
  26.7 7.7 %copy-start.8 = (f32[32]{0:T(128)S(1)}, f32[32]{0:T(128)}, u32[]{:S(2)}) copy-start(f32[32]{0:T(128)} %param.17) | copy-start | bytes 388
  26.7 52.9 %all-to-all-start = ((f32[16,72,512]{2,1,0:T(8,128)}), f32[16,72,512]{2,1,0:T(8,128)S(1)}, u32[]{:S(2)}, u32[]{:S(2)}) async-start(f32[16,72,512]{2,1,0:T(8,128)} %bitcast.33), calls=%async_computation | async-start | bytes 4718592 | tf_op jit(solution)/shard_map/all_to_all | solution.py:145
  84.9 7.9 %copy-start.3 = (f32[2,36,68,128]{3,2,1,0:T(8,128)S(1)}, f32[2,36,68,128]{3,2,1,0:T(8,128)}, u32[]{:S(2)}) copy-start(f32[2,36,68,128]{3,2,1,0:T(8,128)} %broadcast_multiply_fusion.1) | copy-start | bytes 7520260
  84.9 6.6 %collective-permute-start.3 = (f32[2,36,2,128]{3,2,1,0:T(2,128)S(1)}, f32[2,36,2,128]{3,2,1,0:T(2,128)S(1)}, u32[]{:S(2)}, u32[]{:S(2)}) collective-permute-start(f32[2,36,2,128]{3,2,1,0:T(2,128)S(1)} %get-tuple-element.22), channel_id=1, source_target_pairs={{1,0},{3,2},{5,4},{7,6},{9,8},{11,10},{13,12},{15,14},{17,16},{19,... | collective-permute-start | bytes 221192 | tf_op jit(solution)/shard_map/ppermute | solution.py:18
  86.6 6.1 %collective-permute-start.2 = (f32[2,36,2,128]{3,2,1,0:T(2,128)S(1)}, f32[2,36,2,128]{3,2,1,0:T(2,128)S(1)}, u32[]{:S(2)}, u32[]{:S(2)}) collective-permute-start(f32[2,36,2,128]{3,2,1,0:T(2,128)S(1)} %get-tuple-element.21), channel_id=1, source_target_pairs={{0,1},{2,3},{4,5},{6,7},{8,9},{10,11},{12,13},{14,15},{16,17},{18,... | collective-permute-start | bytes 221192 | tf_op jit(solution)/shard_map/ppermute | solution.py:17
  95.7 1.7 copy-start.4
  102.3 1.7 copy-start.2
  106.6 5.5 %collective-permute-start.4 = (f32[2,36,2,128]{3,2,1,0:T(2,128)S(1)}, f32[2,36,2,128]{3,2,1,0:T(2,128)S(1)}, u32[]{:S(2)}, u32[]{:S(2)}) collective-permute-start(f32[2,36,2,128]{3,2,1,0:T(2,128)S(1)} %get-tuple-element.17), channel_id=1, source_target_pairs={{0,1},{2,3},{4,5},{6,7},{8,9},{10,11},{12,13},{14,15},{16,17},{18,... | collective-permute-start | bytes 221192 | tf_op jit(solution)/shard_map/ppermute | solution.py:17
  110.7 5.1 %collective-permute-start.5 = (f32[2,36,2,128]{3,2,1,0:T(2,128)S(1)}, f32[2,36,2,128]{3,2,1,0:T(2,128)S(1)}, u32[]{:S(2)}, u32[]{:S(2)}) collective-permute-start(f32[2,36,2,128]{3,2,1,0:T(2,128)S(1)} %get-tuple-element.18), channel_id=1, source_target_pairs={{1,0},{3,2},{5,4},{7,6},{9,8},{11,10},{13,12},{15,14},{17,16},{19,... | collective-permute-start | bytes 221192 | tf_op jit(solution)/shard_map/ppermute | solution.py:18
  125.9 3.1 %collective-permute-start.6 = (f32[2,36,2,128]{3,2,1,0:T(2,128)S(1)}, f32[2,36,2,128]{3,2,1,0:T(2,128)S(1)}, u32[]{:S(2)}, u32[]{:S(2)}) collective-permute-start(f32[2,36,2,128]{3,2,1,0:T(2,128)S(1)} %get-tuple-element.13), channel_id=1, source_target_pairs={{0,1},{2,3},{4,5},{6,7},{8,9},{10,11},{12,13},{14,15},{16,17},{18,... | collective-permute-start | bytes 221192 | tf_op jit(solution)/shard_map/ppermute | solution.py:17
  127.5 5.1 %collective-permute-start.7 = (f32[2,36,2,128]{3,2,1,0:T(2,128)S(1)}, f32[2,36,2,128]{3,2,1,0:T(2,128)S(1)}, u32[]{:S(2)}, u32[]{:S(2)}) collective-permute-start(f32[2,36,2,128]{3,2,1,0:T(2,128)S(1)} %get-tuple-element.14), channel_id=1, source_target_pairs={{1,0},{3,2},{5,4},{7,6},{9,8},{11,10},{13,12},{15,14},{17,16},{19,... | collective-permute-start | bytes 221192 | tf_op jit(solution)/shard_map/ppermute | solution.py:18
  148.0 70.7 %copy-start.1 = (bf16[1152,1152]{1,0:T(8,128)(2,1)S(1)}, bf16[1152,1152]{1,0:T(8,128)(2,1)}, u32[]{:S(2)}) copy-start(bf16[1152,1152]{1,0:T(8,128)(2,1)} %param.12) | copy-start | bytes 7962628
where the time goes:
time: 219 us
  blocking collectives  69.3 us (32%)
  waiting for transfers between devices  47.7 us (22%)
  other arithmetic  40.1 us (18%)
  local copies, waits for them, and re-layouts  27 us (12%)
  starting transfers between devices  26.7 us (12%)
  matrix products  7.46 us (3%)
    all_to_all x1, blocking collectives, per_device(): lax.all_to_all(flattened, 'comp', split_axis=1, concat_axis=0, tiled=True)  69.3 us
    all_to_all x1, waiting for transfers between devices, per_device(): lax.all_to_all(source_terms(spectrum, wind_field, coupling, growth, dissi...  38.7 us
    mul x9, other arithmetic, face_flux(): return courant * (central - (1.0 - courant * courant) / 6.0 * curvature)  26.2 us
    ppermute x4, starting transfers between devices, extended(): before = lax.ppermute(last, axis, up)  14.1 us
    ppermute x4, waiting for transfers between devices, extended(): after = lax.ppermute(leading, axis, down)  7.62 us
    dot_general x1, matrix products, source_terms(): jnp.dot(coupling, energy.astype(jnp.bfloat16), preferred_element_type=jnp...  7.01 us
    all_to_all x1, starting transfers between devices, per_device(): lax.all_to_all(source_terms(spectrum, wind_field, coupling, growth, dissi...  6.91 us
    ppermute x4, starting transfers between devices, extended(): after = lax.ppermute(leading, axis, down)  5.65 us
  transfers between devices with their start and end apart: 9, of which 6 were waited for; matrix products, arithmetic and copies ran while one was open for 13% of the time, Pallas kernels for 0%

commit v1 on v0

v1 whole, which is shorter than its diff:
```python
import functools

import jax
import jax.numpy as jnp
import numpy as np
from jax import lax
from jax.experimental import pallas as pl
from jax.experimental.pallas import tpu as pltpu
from jax.sharding import PartitionSpec as P

ND = 36
LANES = 128
TILE = 8
CHUNKS = 2
BLOCKS = ("comp", "space")

ANGLES = 2.0 * np.pi * np.arange(ND) / ND
COS = [float(v) for v in np.cos(ANGLES)]
SIN = [float(v) for v in np.sin(ANGLES)]
HALF = 2.0 * np.pi * (np.arange(ND) + 0.5) / ND
SPREAD = float(np.cos(np.pi / ND))
COS_FACE = [float(v) * SPREAD for v in np.cos(HALF)]
SIN_FACE = [float(v) * SPREAD for v in np.sin(HALF)]

UPWARD = list(range(28, 36)) + list(range(0, 10))
DOWNWARD = list(range(10, 28))
CLASSES = 10

ONE = ND + 18
TWO = 2 * ND + 22 + 18
THIRD = 2 * ND
FOURTH = THIRD + 22


def places_one(row, d):
    up = d in UPWARD
    slot = (d + 8) % ND if up else d - 10
    if row == 3:
        return [(0, d)]
    if row == 0:
        return [(1, d)]
    if row == 2:
        return [(0, ND + slot)] if up else [(2, 18 + slot)]
    return [(2, slot)] if up else [(1, ND + slot)]


def places_two(row, d):
    up = d in UPWARD
    found = [(0, (3 - row) * ND + d)] if row >= 2 else [(1, row * ND + d)]
    if row == 1 and (d + 10) % ND < 22:
        found.append((0, THIRD + (d + 10) % ND))
    if row == 2 and 8 <= d < 30:
        found.append((1, THIRD + d - 8))
    if row == 0 and up:
        found.append((0, FOURTH + (d + 8) % ND))
    if row == 3 and not up:
        found.append((1, FOURTH + d - 10))
    return found


def pick_row(strip, row):
    index = lax.broadcasted_iota(jnp.int32, strip.shape, 0)
    return jnp.sum(jnp.where(index == row, strip, 0.0), axis=0, keepdims=True)


def column_of(row_values, first, count):
    size = row_values.shape[1]
    shape = (count, size)
    chosen = (
        lax.broadcasted_iota(jnp.int32, shape, 0) + first
        == lax.broadcasted_iota(jnp.int32, shape, 1)
    )
    return jnp.sum(jnp.where(chosen, row_values, 0.0), axis=1, keepdims=True)


def fetch(pairs, sems):
    copies = [pltpu.make_async_copy(src, dst, sems.at[i]) for i, (src, dst) in enumerate(pairs)]
    for copy in copies:
        copy.start()
    return copies


def run_copies(pairs, sems):
    for copy in fetch(pairs, sems):
        copy.wait()


def by_parity(odd, even_way, odd_way):
    pl.when(jnp.logical_not(odd))(even_way)
    pl.when(odd)(odd_way)


def source_kernel(chunk, freqs, last, comps, *refs):
    refs = list(refs)
    rows = 4
    block = refs.pop(0)[0]
    spectrum, wind, coupling, growth_in, dissipation_in, mask_in, index_in = (
        refs.pop(0) for _ in range(7)
    )
    if last:
        tables_in = [refs.pop(0) for _ in range(3)]
    even_out, odd_out = refs.pop(0), refs.pop(0)
    if last:
        kit_out = refs.pop(0)
    outs = [refs.pop(0) for _ in range(2)]
    spec, wind_ref, operator, growth_ref, dissipation_ref, rounded, mixed = refs[:7]
    mask_ref, index_ref, sems = refs[7:10]
    span = freqs * ND
    pairs = [(spectrum.at[:, pl.ds(r * LANES, LANES)], spec.at[r]) for r in range(rows)]
    pairs += [
        (coupling.at[pl.ds(chunk * span, span), :], operator),
        (wind, wind_ref),
        (growth_in, growth_ref),
        (dissipation_in, dissipation_ref),
        (mask_in, mask_ref),
        (index_in, index_ref),
    ]
    if last:
        kit = refs[10]
        depths_ref, speed_ref, refraction_ref = refs[11:]
        pairs += list(zip(tables_in, (depths_ref, speed_ref, refraction_ref)))
    copies = fetch(pairs, sems)
    for r in range(rows):
        copies[r].wait()
        rounded[:, r * LANES : (r + 1) * LANES] = spec[r].astype(jnp.bfloat16)
    for copy in copies[rows:]:
        copy.wait()
    nonlinear = jnp.dot(operator[...], rounded[...], preferred_element_type=jnp.float32)
    for r in range(rows):
        mixed[r] = nonlinear[:, r * LANES : (r + 1) * LANES]
    components = spec.shape[1]
    growth = column_of(growth_ref[...], chunk * freqs, freqs)
    dissipation = column_of(dissipation_ref[...], chunk * freqs, freqs)
    tiles = freqs // TILE
    for r in range(rows):
        average = jnp.sum(spec[r], axis=0, keepdims=True) * (1.0 / components)
        limited = average / (average + 1.0)
        wind_x = jnp.broadcast_to(wind_ref[0:1, r * LANES : (r + 1) * LANES], (TILE, LANES))
        wind_y = jnp.broadcast_to(wind_ref[1:2, r * LANES : (r + 1) * LANES], (TILE, LANES))
        grow = []
        damp = []
        for t in range(tiles):
            part = slice(t * TILE, (t + 1) * TILE)
            grow.append(jnp.broadcast_to(growth[part], (TILE, LANES)))
            damp.append(dissipation[part] * limited)
        for d in range(ND):
            forcing = jnp.maximum(COS[d] * wind_x + SIN[d] * wind_y, 0.0)
            squared = forcing * forcing
            for t in range(tiles):
                base = (chunk * freqs + t * TILE) * ND + d
                energy = spec[r, pl.ds(base, TILE, stride=ND), :]
                extra = mixed[r, pl.ds(t * TILE * ND + d, TILE, stride=ND), :]
                value = energy + (grow[t] * squared - damp[t]) * energy + 0.25 * extra
                for which, slot in places_two(r, d):
                    outs[which][slot, t * TILE : (t + 1) * TILE, :] = value
    first = lax.rem(block, comps) * rows
    mask = mask_ref[...].astype(jnp.float32)
    index = index_ref[...].astype(jnp.float32)
    leaving = []
    if chunk == 0:
        for out, row in ((outs[0], first + rows - 3), (outs[1], first)):
            for k in range(3):
                out[TWO, k : k + 1, :] = pick_row(mask, row + k)
                out[TWO, 3 + k : 4 + k, :] = pick_row(index, row + k)
            out[TWO, 6:, :] = jnp.zeros((freqs - 6, LANES), jnp.float32)
    if last:
        count, levels = speed_ref.shape
        kit[...] = jnp.zeros_like(kit)
        kit[:count, :levels] = speed_ref[...]
        kit[count : 2 * count, :levels] = refraction_ref[...]
        kit[2 * count : 2 * count + 1, :levels] = depths_ref[...]
        for r in range(rows):
            kit[2 * count + TILE + r, :] = pick_row(mask, first + r)[0]
            kit[2 * count + TILE + rows + r, :] = pick_row(index, first + r)[0]
        leaving.append((kit, kit_out))
    by_parity(
        lax.rem(block, 2) == 1,
        lambda: run_copies([(outs[0], even_out), (outs[1], odd_out)] + leaving, sems),
        lambda: run_copies([(outs[1], even_out), (outs[0], odd_out)] + leaving, sems),
    )


def weights(courant):
    half = 0.5 * courant
    square = courant * half
    curve = (half - courant * square) * (1.0 / 3.0)
    rising = half + square
    falling = half - square
    return rising + (curve + curve), falling - curve, curve


def coast_kernel(
    count, block_ref, even_ref, odd_ref, kit_ref, face_x, face_y, turn_ref, land_ref, slope_by
):
    rows = 4
    tables = kit_ref[: 2 * count + TILE, :]
    odd = lax.rem(block_ref[0], 2) == 1
    even, odds = even_ref[TWO, :TILE, :], odd_ref[TWO, :TILE, :]
    low, high = jnp.where(odd, even, odds), jnp.where(odd, odds, even)
    masks = [low[k : k + 1] for k in range(3)]
    levels = [low[3 + k : 4 + k] for k in range(3)]
    for r in range(rows):
        row = 2 * count + TILE + r
        masks.append(kit_ref[row : row + 1, :])
        levels.append(kit_ref[row + rows : row + rows + 1, :])
    masks += [high[k : k + 1] for k in range(3)]
    levels += [high[3 + k : 4 + k] for k in range(3)]
    wanted = jnp.concatenate(levels, axis=1)
    entry = lax.broadcasted_iota(jnp.int32, (LANES, wanted.shape[1]), 0).astype(jnp.float32)
    onehot = (entry == wanted).astype(jnp.float32)
    looked = jnp.dot(
        tables, onehot, precision=lax.Precision.HIGHEST, preferred_element_type=jnp.float32
    )
    speeds = looked[:count]
    turns = looked[count : 2 * count]
    depth = looked[2 * count : 2 * count + 1]

    def at(values, i):
        return values[:, i * LANES : (i + 1) * LANES]

    heights = [at(depth, i) * masks[i] for i in range(rows + 6)]
    for face in range(rows + 5):
        weight = 0.5 * (masks[face] * masks[face + 1])
        face_x[face] = (at(speeds, face) + at(speeds, face + 1)) * weight
    lane = lax.broadcasted_iota(jnp.int32, (1, LANES), 1)
    for r in range(rows + 4):
        mask = masks[r + 1]
        after = jnp.where(lane < LANES - 1, pltpu.roll(mask, LANES - 1, 1), 0.0)
        speed = at(speeds, r + 1)
        face_y[r] = (speed + pltpu.roll(speed, LANES - 1, 1)) * (0.5 * (mask * after))
        slope_x = 0.5 * (heights[r + 2] - heights[r])
        height = heights[r + 1]
        next_height = jnp.where(lane < LANES - 1, pltpu.roll(height, LANES - 1, 1), 0.0)
        last_height = jnp.where(lane > 0, pltpu.roll(height, 1, 1), 0.0)
        slope_y = 0.5 * (next_height - last_height)
        turn = at(turns, r + 1)
        slope_by[2 * r] = turn * slope_x
        slope_by[2 * r + 1] = turn * slope_y
        land_ref[r] = jnp.broadcast_to(mask, (TILE, LANES))

    @pl.loop(0, count // TILE)
    def _(t):
        part = pl.ds(pl.multiple_of(t * TILE, TILE), TILE)

        @pl.loop(0, rows + 4)
        def _(r):
            turn_x = slope_by[2 * r, part, :]
            turn_y = slope_by[2 * r + 1, part, :]
            for d in range(ND // 2):
                turn_ref[t, r * (ND // 2) + d] = turn_x * SIN_FACE[d] - turn_y * COS_FACE[d]


def shift_rows_columns(
    part, first, last, cells_of, moved, x_ref, y_ref, base, trig, j, members, put
):
    along_x = {
        k: weights(x_ref[base + k, part, :] * trig[0, j]) for k in range(first, last + 2)
    }
    for i, (d, _, up, _) in enumerate(members):
        cell = functools.partial(cells_of, d)
        if up:
            cells = {r: cell(r) for r in range(first - 2, last + 2)}
            faces = {
                k: a * cells[k - 1] + b * cells[k] - c * cells[k - 2]
                for k, (a, b, c) in along_x.items()
            }
            for r in range(first, last + 1):
                moved[i, r - first] = cells[r] - (faces[r + 1] - faces[r])
        else:
            cells = {r: cell(r) for r in range(first - 1, last + 3)}
            faces = {
                k: a * cells[k] + b * cells[k - 1] - c * cells[k + 1]
                for k, (a, b, c) in along_x.items()
            }
            for r in range(first, last + 1):
                moved[i, r - first] = cells[r] + (faces[r + 1] - faces[r])
    lanes = lax.broadcasted_iota(jnp.int32, (TILE, LANES), 1)
    not_first = (lanes != 0).astype(jnp.float32)
    not_last = (lanes != LANES - 2).astype(jnp.float32)
    for r in range(first, last + 1):
        near, far, curve = weights(y_ref[base + r, part, :] * trig[1, j])
        curve_up = curve * not_first
        curve_down = curve * not_last
        for i, (_, d, _, to_higher) in enumerate(members):
            here = moved[i, r - first]
            after = pltpu.roll(here, LANES - 1, 1)
            if to_higher:
                before = pltpu.roll(here, 1, 1)
                face = near * here + far * after - curve_up * before
                result = here - (face - pltpu.roll(face, 1, 1))
            else:
                beyond = pltpu.roll(here, LANES - 2, 1)
                face = near * after + far * here - curve_down * beyond
                result = here + (face - pltpu.roll(face, 1, 1))
            put(r, d, result)


def every_class(tiles, one_class):
    @pl.loop(0, CLASSES)
    def _(j):
        single = jnp.logical_or(j == 0, j == 9)
        rising = jnp.where(j == 0, 0, ND - j)
        members = [
            (j, j, True, True),
            (rising, jnp.where(single, ND, rising), True, False),
            (18 - j, jnp.where(j == 9, ND, 18 - j), False, True),
            (18 + j, jnp.where(j == 0, ND, 18 + j), False, False),
        ]
        for t in range(tiles):
            one_class(t, j, members)


def turn_rows(jobs):
    half_turn = ND // 2

    def slope(read, i):
        return read((i + 1) % ND) - read(i % ND)

    def pair(read, turning, d, known):
        courant = turning(d)
        half = 0.5 * courant
        spread = (1.0 / 3.0) - courant * (courant * (1.0 / 3.0))
        positive = courant >= 0.0
        faces = []
        following = []
        for side in range(2):
            own = d + side * half_turn
            rise, bend = known[side]
            next_rise = slope(read, own + 1)
            next_bend = next_rise - rise
            total = read(own) + read((own + 1) % ND)
            if side == 0:
                chosen = jnp.where(positive, bend, next_bend)
                faces.append(half * ((total - courant * rise) - spread * chosen))
            else:
                chosen = jnp.where(positive, next_bend, bend)
                faces.append(half * ((total + courant * rise) - spread * chosen))
            following.append((next_rise, next_bend))
        return faces, following

    def known_at(read, d):
        found = []
        for side in range(2):
            own = d + side * half_turn
            rise = slope(read, own)
            found.append((rise, rise - slope(read, own - 1)))
        return found

    states = []
    for read, turning, _, _ in jobs:
        ends, following = pair(read, turning, half_turn - 1, known_at(read, half_turn - 1))
        states.append((ends, [0.0 - ends[1], 0.0 - ends[0]], [following[1], following[0]]))
    for d in range(half_turn):
        for i, (read, turning, land, put) in enumerate(jobs):
            ends, previous, known = states[i]
            if d == half_turn - 1:
                current = ends
            else:
                current, known = pair(read, turning, d, known)
            put(d, (read(d) - (current[0] - previous[0])) * land)
            own = d + half_turn
            put(own, (read(own) + (current[1] - previous[1])) * land)
            states[i] = (ends, current, known)


def set_trig(trig):
    for j in range(CLASSES):
        trig[0, j] = abs(COS[j])
        trig[1, j] = abs(SIN[j])


def two_steps_kernel(chunk, freqs, *refs):
    block_ref, even_own, odd_own, even_ref, odd_ref, x_ref, y_ref, turn_ref, land_ref = refs[:9]
    even_out, odd_out, rest_out = refs[9:12]
    cells, work, moved, trig = refs[12:]
    odd = lax.rem(block_ref[0], 2) == 1
    tiles = freqs // TILE
    half_turn = ND // 2
    set_trig(trig)
    parts = [slice(t * TILE, (t + 1) * TILE) for t in range(tiles)]

    def gather(up_ref, down_ref, low_ref, high_ref):
        @pl.loop(0, ND)
        def _(d):
            for t, part in enumerate(parts):
                for k in range(2):
                    cells[0, t, 3 - k, d] = low_ref[k * ND + d, part, :]
                    cells[0, t, 4 + k, d] = down_ref[k * ND + d, part, :]
                    cells[0, t, 7 - k, d] = up_ref[k * ND + d, part, :]
                    cells[0, t, 8 + k, d] = high_ref[k * ND + d, part, :]

        @pl.loop(0, 22)
        def _(i):
            for t, part in enumerate(parts):
                cells[0, t, 1, lax.rem(i + 26, ND)] = low_ref[THIRD + i, part, :]
                cells[0, t, 10, i + 8] = high_ref[THIRD + i, part, :]

        @pl.loop(0, 18)
        def _(i):
            for t, part in enumerate(parts):
                cells[0, t, 0, lax.rem(i + 28, ND)] = low_ref[FOURTH + i, part, :]
                cells[0, t, 11, i + 10] = high_ref[FOURTH + i, part, :]

    by_parity(
        odd,
        lambda: gather(even_own, odd_own, odd_ref, even_ref),
        lambda: gather(odd_own, even_own, even_ref, odd_ref),
    )

    @pl.loop(0, 3)
    def _(stage):
        source = stage // 2
        base = jnp.where(stage == 0, 2, jnp.where(stage == 1, 6, 4))

        def one_class(t, j, members):
            def cell(d, r):
                return cells[source, t, base + r, d]

            def put(r, d, value):
                work[t, r, d] = value

            table = pl.ds(chunk * freqs + t * TILE, TILE)
            shift_rows_columns(
                table, 0, 3, cell, moved.at[t], x_ref, y_ref, base - 2, trig, j, members, put
            )

        every_class(tiles, one_class)

        @pl.loop(0, tiles * 4)
        def _(i):
            t = i // 4
            r = lax.rem(i, 4)

            def put(d, value):
                cells[1 - source, t, base + r, d] = value

            turn_rows(
                [
                    (
                        lambda d: work[t, r, d],
                        lambda d: turn_ref[chunk * tiles + t, (base - 2 + r) * half_turn + d],
                        land_ref[base - 2 + r],
                        put,
                    )
                ]
            )

    def hand_out(up_out, down_out):
        @pl.loop(0, ND)
        def _(d):
            for t, part in enumerate(parts):
                up_out[d, part, :] = cells[0, t, 7, d]
                down_out[d, part, :] = cells[0, t, 4, d]

        @pl.loop(0, half_turn)
        def _(i):
            upward = lax.rem(i + 28, ND)
            for t, part in enumerate(parts):
                up_out[ND + i, part, :] = cells[0, t, 6, upward]
                down_out[ND + i, part, :] = cells[0, t, 5, i + 10]
                rest_out[i, part, :] = cells[0, t, 5, upward]
                rest_out[half_turn + i, part, :] = cells[0, t, 6, i + 10]

    by_parity(odd, lambda: hand_out(even_out, odd_out), lambda: hand_out(odd_out, even_out))


def last_step_kernel(chunk, freqs, *refs):
    refs = list(refs)
    odd = lax.rem(refs.pop(0)[0], 2) == 1
    even_own, odd_own, rest_ref, even_ref, odd_ref = (refs.pop(0) for _ in range(5))
    x_ref, y_ref, turn_ref, land_ref = (refs.pop(0) for _ in range(4))
    if chunk:
        refs.pop(0)
    out_ref, cells, work, moved, packed, trig, sems = refs
    rows = 4
    tiles = freqs // TILE
    half_turn = ND // 2
    span = freqs * ND
    set_trig(trig)
    parts = [slice(t * TILE, (t + 1) * TILE) for t in range(tiles)]

    def gather(up_ref, down_ref, low_ref, high_ref):
        @pl.loop(0, ND)
        def _(d):
            for t, part in enumerate(parts):
                cells[t, 1, d] = low_ref[d, part, :]
                cells[t, 2, d] = down_ref[d, part, :]
                cells[t, 5, d] = up_ref[d, part, :]
                cells[t, 6, d] = high_ref[d, part, :]

        @pl.loop(0, half_turn)
        def _(i):
            upward = lax.rem(i + 28, ND)
            for t, part in enumerate(parts):
                cells[t, 0, upward] = low_ref[ND + i, part, :]
                cells[t, 3, upward] = rest_ref[i, part, :]
                cells[t, 4, upward] = up_ref[ND + i, part, :]
                cells[t, 3, i + 10] = down_ref[ND + i, part, :]
                cells[t, 4, i + 10] = rest_ref[half_turn + i, part, :]
                cells[t, 7, i + 10] = high_ref[ND + i, part, :]

    by_parity(
        odd,
        lambda: gather(even_own, odd_own, odd_ref, even_ref),
        lambda: gather(odd_own, even_own, even_ref, odd_ref),
    )

    def only_pass(t, j, members):
        def cell(d, r):
            return cells[t, r + 2, d]

        def put(r, d, value):
            work[t, r, d] = value

        table = pl.ds(chunk * freqs + t * TILE, TILE)
        shift_rows_columns(
            table, 0, 3, cell, moved.at[t], x_ref, y_ref, 2, trig, j, members, put
        )

    every_class(tiles, only_pass)

    @pl.loop(0, tiles * 4)
    def _(i):
        t = i // 4
        r = lax.rem(i, 4)

        def put(d, value):
            packed[r, pl.ds(t * (TILE * ND) + d, TILE, stride=ND), :] = value

        turn_rows(
            [
                (
                    lambda d: work[t, r, d],
                    lambda d: turn_ref[chunk * tiles + t, (r + 2) * half_turn + d],
                    land_ref[r + 2],
                    put,
                )
            ]
        )

    run_copies(
        [
            (packed.at[r], out_ref.at[pl.ds(chunk * span, span), pl.ds(r * LANES, LANES)])
            for r in range(rows)
        ],
        sems,
    )


def cost(flops, size):
    return pl.CostEstimate(flops=flops, bytes_accessed=size, transcendentals=0)


def params(limit):
    return pltpu.CompilerParams(vmem_limit_bytes=limit * 1024 * 1024)


def per_device(
    spectrum,
    wind_field,
    coupling,
    growth,
    dissipation,
    group_speed,
    refraction,
    depths,
    sea_mask,
    depth_index,
):
    components, points = spectrum.shape
    nfreq = growth.shape[0]
    levels = depths.shape[0]
    rows = points // LANES
    freqs = nfreq // CHUNKS
    span = freqs * ND
    comps, strips = lax.axis_size("comp"), lax.axis_size("space")
    order = [c * strips + s for s in range(strips) for c in range(comps)]
    steps = list(zip(order[:-1], order[1:]))
    even_swaps = [swap for i, j in steps[0::2] for swap in ((i, j), (j, i))]
    odd_swaps = [swap for i, j in steps[1::2] for swap in ((i, j), (j, i))]
    block_index = lax.axis_index("space") * comps + lax.axis_index("comp")
    block_index = block_index.astype(jnp.int32).reshape(1)
    scalar = pl.BlockSpec(memory_space=pltpu.SMEM)
    near = pl.BlockSpec(memory_space=pltpu.VMEM)
    far = pl.BlockSpec(memory_space=pltpu.HBM)
    growth = growth.reshape(1, nfreq)
    dissipation = dissipation.reshape(1, nfreq)
    depths = depths.reshape(1, levels)

    def block(*shape):
        return jax.ShapeDtypeStruct(shape, jnp.float32)

    def like(array):
        return pltpu.VMEM(array.shape, array.dtype)

    def tiles(count):
        return block(count, freqs, LANES)

    def source(chunk):
        last = chunk == CHUNKS - 1
        shapes = [tiles(TWO + (1 if chunk == 0 else 0))] * 2
        operands = [spectrum, wind_field, coupling, growth, dissipation, sea_mask, depth_index]
        scratch = [like(shape) for shape in shapes] + [
            pltpu.VMEM((rows, components, LANES), jnp.float32),
            like(wind_field),
            pltpu.VMEM((span, components), jnp.bfloat16),
            like(growth),
            like(dissipation),
            pltpu.VMEM((components, points), jnp.bfloat16),
            pltpu.VMEM((rows, span, LANES), jnp.float32),
            like(sea_mask),
            like(depth_index),
            pltpu.SemaphoreType.DMA((14,)),
        ]
        if last:
            shapes.append(block(2 * nfreq + 2 * TILE, LANES))
            more = [depths, group_speed, refraction]
            operands += more
            scratch += [like(shapes[2])] + [like(a) for a in more]
        return pl.pallas_call(
            functools.partial(source_kernel, chunk, freqs, last, comps),
            in_specs=[scalar] + [far] * len(operands),
            out_specs=[far] * len(shapes),
            out_shape=shapes,
            scratch_shapes=scratch,
            compiler_params=params(57 if chunk else 63),
            cost_estimate=cost(2 * span * components * points, 4 * components * points),
            name="source_terms",
        )(block_index, *operands)

    def coast(even, odd, kit):
        shapes = [
            block(rows + 5, nfreq, LANES),
            block(rows + 4, nfreq, LANES),
            block(nfreq // TILE, (rows + 4) * (ND // 2), TILE, LANES),
            block(rows + 4, TILE, LANES),
        ]
        return pl.pallas_call(
            functools.partial(coast_kernel, nfreq),
            in_specs=[scalar] + [near] * 3,
            out_specs=[near] * len(shapes),
            out_shape=shapes,
            scratch_shapes=[pltpu.VMEM((2 * (rows + 4), nfreq, LANES), jnp.float32)],
            compiler_params=params(24),
            cost_estimate=cost(ND * rows * nfreq * LANES, 4 * ND * rows * nfreq * LANES),
            name="coast_tables",
        )(block_index, even, odd, kit)

    def exchange(even, odd):
        odd = lax.ppermute(odd, BLOCKS, odd_swaps)
        return lax.ppermute(even, BLOCKS, even_swaps), odd

    work = pltpu.VMEM((freqs // TILE, rows, ND + 1, TILE, LANES), jnp.float32)

    passed = pltpu.VMEM((freqs // TILE, 4, rows, TILE, LANES), jnp.float32)

    trig = pltpu.SMEM((2, CLASSES), jnp.float32)

    def two_steps(chunk, state, halo, tables):
        operands = [block_index, *state, *halo, *tables]
        shapes = [tiles(ONE), tiles(ONE), tiles(ND)]
        return pl.pallas_call(
            functools.partial(two_steps_kernel, chunk, freqs),
            in_specs=[scalar] + [near] * (len(operands) - 1),
            out_specs=[near] * len(shapes),
            out_shape=shapes,
            scratch_shapes=[
                pltpu.VMEM((2, freqs // TILE, rows + 8, ND, TILE, LANES), jnp.float32),
                work,
                passed,
                trig,
            ],
            compiler_params=params(24),
            cost_estimate=cost(3 * 40 * span * points, 4 * 4 * span * points),
            name="two_substeps",
        )(*operands)

    def last_step(chunk, state, halo, tables, out):
        operands = [block_index, *state, *halo, *tables]
        specs = [scalar] + [near] * (len(operands) - 1)
        aliases = {}
        if out is not None:
            aliases = {len(operands): 0}
            operands.append(out)
            specs.append(far)
        return pl.pallas_call(
            functools.partial(last_step_kernel, chunk, freqs),
            in_specs=specs,
            out_specs=far,
            out_shape=block(*spectrum.shape),
            scratch_shapes=[
                pltpu.VMEM((freqs // TILE, rows + 4, ND, TILE, LANES), jnp.float32),
                work,
                passed,
                pltpu.VMEM((rows, span, LANES), jnp.float32),
                trig,
                pltpu.SemaphoreType.DMA((rows,)),
            ],
            input_output_aliases=aliases,
            compiler_params=params(24),
            cost_estimate=cost(40 * span * points, 4 * 4 * span * points),
            name="last_substep",
        )(*operands)

    states = []
    halos = []
    for chunk in range(CHUNKS):
        even, odd, *kit = source(chunk)
        states.append((even, odd))
        halos.append(exchange(even, odd))
    tables = coast(*halos[0], *kit)
    for chunk in range(CHUNKS):
        states[chunk] = two_steps(chunk, states[chunk], halos[chunk], tables)
        halos[chunk] = exchange(*states[chunk][:2])
    out = None
    for chunk in range(CHUNKS):
        out = last_step(chunk, states[chunk], halos[chunk], tables, out)
    return out


def solution(mesh):
    in_specs = (
        P(None, ("comp", "space")),
        P(None, ("comp", "space")),
        P(),
        P(),
        P(),
        P(),
        P(),
        P(),
        P("space", None),
        P("space", None),
    )
    out_specs = P(None, ("comp", "space"))
    return jax.shard_map(
        per_device, mesh=mesh, in_specs=in_specs, out_specs=out_specs, check_vma=False
    )
```

time: 219 us -> 84.7 us (0.39)
  blocking collectives: 69.3 us -> 0 us
  other arithmetic: 40.1 us -> 0 us
  Pallas kernels: 0 us -> 39.2 us
  local copies, waits for them, and re-layouts: 27 us -> 0.8 us
  waiting for transfers between devices: 47.7 us -> 28.1 us
  starting transfers between devices: 26.7 us -> 16 us
  matrix products: 7.46 us -> 0 us
    all_to_all x1 -> x0, blocking collectives: 69.3 us -> none  [per_device(): lax.all_to_all(flattened, 'comp', split_axis=1, concat_axis=0, tiled=True)]
    pallas_call x0 -> x7, Pallas kernels: none -> 39.2 us  [the longest x2 20 us: two_steps(): pl.pallas_call(functools.partial(two_steps_kernel, chunk, freqs), in_spec...]
    all_to_all x1 -> x0, waiting for transfers between devices: 38.7 us -> none  [per_device(): lax.all_to_all(source_terms(spectrum, wind_field, coupling, growth, dissi...]
    mul x21 -> x0, other arithmetic: 33.1 us -> none  [the longest x9 26.2 us: face_flux(): return courant * (central - (1.0 - courant * courant) / 6.0 * curvature)]
    ppermute x8, waiting for transfers between devices: 9.02 us -> 28.1 us  [the longest x4 28.1 us: exchange(): odd = lax.ppermute(odd, BLOCKS, odd_swaps)]
    dot_general x2 -> x0, matrix products: 7.46 us -> none  [the longest x1 7.01 us: source_terms(): jnp.dot(coupling, energy.astype(jnp.bfloat16), preferred_element_type=jnp...]
    all_to_all x1 -> x0, starting transfers between devices: 6.91 us -> none  [per_device(): lax.all_to_all(source_terms(spectrum, wind_field, coupling, growth, dissi...]
    all_to_all x3 -> x0, local copies, waits for them, and re-layouts: 6.59 us -> none  [the longest x2 3.81 us: per_device(): lax.all_to_all(flattened, 'comp', split_axis=1, concat_axis=0, tiled=True)]
  transfers between devices with their start and end apart: 9 -> 8, of which waited for: 6 -> 2; matrix products, arithmetic and copies ran while one was open for 13% -> 0% of each run, Pallas kernels for 0% -> 36%
where the time goes in v1:
time: 84.7 us; the launch traced here: 84.3 us
  Pallas kernels  39.2 us (46%)
  waiting for transfers between devices  28.1 us (33%)
  starting transfers between devices  16 us (19%)
    ppermute x4, waiting for transfers between devices, exchange(): odd = lax.ppermute(odd, BLOCKS, odd_swaps)  28.1 us
    pallas_call x2, Pallas kernels, two_steps(): pl.pallas_call(functools.partial(two_steps_kernel, chunk, freqs), in_spec...  20 us
    ppermute x4, starting transfers between devices, exchange(): odd = lax.ppermute(odd, BLOCKS, odd_swaps)  15.7 us
    pallas_call x2, Pallas kernels, source(): pl.pallas_call(functools.partial(source_kernel, chunk, freqs, last, comps...  9.4 us
    pallas_call x2, Pallas kernels, last_step(): pl.pallas_call(functools.partial(last_step_kernel, chunk, freqs), in_spec...  8.93 us
  transfers between devices with their start and end apart: 8, of which 2 were waited for; matrix products, arithmetic and copies ran while one was open for 0% of the time, Pallas kernels for 36%

profile of v1, /device:TPU:1, one launch (start us, length us, event | category | flops | bytes accessed | tf_op | source)
XLA Modules:
  0.0 84.3 jit_solution(11776084843167072494)
XLA Ops:
  0.0 4.6 %source_terms.3 = (f32[113,16,128]{2,1,0:T(8,128)}, f32[113,16,128]{2,1,0:T(8,128)}) custom-call(s32[1]{0:T(128)} %bitcast.refs_0_.block_ref, f32[1152,512]{1,0:T(8,128)} %refs_1_.3, f32[2,512]{1,0:T(2,128)} %refs_2_.3, bf16[1152,1152]{1,0:T(8,128)(2,1)} %refs_3_.3, f32[1,32]{1,0:T(1,128)} %bitcast.4, f32[1,32]{1,0:T(1,128)} %bitcast.6, s32[64,128]{1,0:T(8,128)} %refs_6_.3, ...), custom_call_target="tpu_custom_call" | custom-call | flops 679477248 | bytes 2359296 | tf_op jit(solution)/shard_map/source_terms/pallas_call | solution.py:620
  4.6 0.1 collective-permute-start.2
  4.7 4.5 %collective-permute-start.3 = (f32[113,16,128]{2,1,0:T(8,128)}, f32[113,16,128]{2,1,0:T(8,128)S(1)}, u32[]{:S(2)}, u32[]{:S(2)}) collective-permute-start(f32[113,16,128]{2,1,0:T(8,128)} %get-tuple-element.23.refs_2_), channel_id=1, source_target_pairs={{2,4},{4,2},{6,8},{8,6},{10,12},{12,10},{14,16},{16,14},{18,20},{2... | collective-permute-start | bytes 2777096 | tf_op jit(solution)/shard_map/ppermute | solution.py:650
  9.2 0.0 copy-start
  9.2 0.0 copy-start.1
  9.2 4.8 %source_terms.2 = (f32[112,16,128]{2,1,0:T(8,128)}, f32[112,16,128]{2,1,0:T(8,128)}, f32[80,128]{1,0:T(8,128)}) custom-call(s32[1]{0:T(128)} %bitcast.refs_0_.block_ref, f32[1152,512]{1,0:T(8,128)} %refs_1_.3, f32[2,512]{1,0:T(2,128)} %refs_2_.3, bf16[1152,1152]{1,0:T(8,128)(2,1)} %refs_3_.3, f32[1,32]{1,0:T(1,128)} %bitcast.5, f32[1,32]{1,0:T(1,128)} %bitcast.7, ...), custom_call_target="tpu_custom_call" | custom-call | flops 679477248 | bytes 2359296 | tf_op jit(solution)/shard_map/source_terms/pallas_call | solution.py:620
  14.0 0.1 collective-permute-start
  14.1 3.5 %collective-permute-start.1 = (f32[112,16,128]{2,1,0:T(8,128)}, f32[112,16,128]{2,1,0:T(8,128)S(1)}, u32[]{:S(2)}, u32[]{:S(2)}) collective-permute-start(f32[112,16,128]{2,1,0:T(8,128)} %get-tuple-element.21.refs_2_), channel_id=1, source_target_pairs={{2,4},{4,2},{6,8},{8,6},{10,12},{12,10},{14,16},{16,14},{18,20},{2... | collective-permute-start | bytes 2752520 | tf_op jit(solution)/shard_map/ppermute | solution.py:650
  17.7 0.0 collective-permute-done.2.even_ref.refs_3_
  17.7 22.6 %collective-permute-done.3.odd_ref.refs_4_ = f32[113,16,128]{2,1,0:T(8,128)S(1)} collective-permute-done((f32[113,16,128]{2,1,0:T(8,128)}, f32[113,16,128]{2,1,0:T(8,128)S(1)}, u32[]{:S(2)}, u32[]{:S(2)}) %collective-permute-start.3) | collective-permute-done | bytes 925728 | tf_op jit(solution)/shard_map/ppermute | solution.py:650
  40.3 0.0 copy-start.4
  40.3 0.8 copy-done.4
  41.1 0.9 %coast_tables.1 = (f32[9,32,128]{2,1,0:T(8,128)S(1)}, f32[8,32,128]{2,1,0:T(8,128)S(1)}, f32[4,144,8,128]{3,2,1,0:T(8,128)S(1)}, f32[8,8,128]{2,1,0:T(8,128)S(1)}) custom-call(s32[1]{0:T(128)} %bitcast.refs_0_.block_ref, f32[113,16,128]{2,1,0:T(8,128)S(1)} %collective-permute-done.2.even_ref.refs_3_, ...), custom_call_target="tpu_custom_call" | custom-call | flops 589824 | bytes 2359296 | tf_op jit(solution)/shard_map/coast_tables/pallas_call | solution.py:638
  42.0 0.0 copy-done
  42.1 0.0 copy-done.1
  42.1 0.0 copy-start.2
  42.1 0.0 copy-start.3
  42.1 10.0 %two_substeps.3 = (f32[54,16,128]{2,1,0:T(8,128)S(1)}, f32[54,16,128]{2,1,0:T(8,128)S(1)}, f32[36,16,128]{2,1,0:T(8,128)S(1)}) custom-call(s32[1]{0:T(128)} %bitcast.refs_0_.block_ref, f32[113,16,128]{2,1,0:T(8,128)S(1)} %copy-done, f32[113,16,128]{2,1,0:T(8,128)S(1)} %copy-done.1, f32[113,16,128]{2,1,0:T(8,128)S(1)} %collective-permute-done.2.even_ref.refs_3_, ...), custom_call_target="tpu_custom_call" | custom-call | flops 35389440 | bytes 4718592 | tf_op jit(solution)/shard_map/two_substeps/pallas_call | solution.py:662
  52.1 0.1 collective-permute-start.6
  52.2 3.6 %collective-permute-start.7 = (f32[54,16,128]{2,1,0:T(8,128)S(1)}, f32[54,16,128]{2,1,0:T(8,128)S(1)}, u32[]{:S(2)}, u32[]{:S(2)}) collective-permute-start(f32[54,16,128]{2,1,0:T(8,128)S(1)} %get-tuple-element.33.refs_2_), channel_id=1, source_target_pairs={{2,4},{4,2},{6,8},{8,6},{10,12},{12,10},{14,16},{16,14},{18,20},{2... | collective-permute-start | bytes 1327112 | tf_op jit(solution)/shard_map/ppermute | solution.py:650
  55.8 0.0 collective-permute-done.refs_3_
  55.8 0.0 collective-permute-done.1.refs_4_
  55.8 0.0 copy-done.2
  55.8 0.0 copy-done.3
  55.9 10.0 %two_substeps.2 = (f32[54,16,128]{2,1,0:T(8,128)S(1)}, f32[54,16,128]{2,1,0:T(8,128)S(1)}, f32[36,16,128]{2,1,0:T(8,128)S(1)}) custom-call(s32[1]{0:T(128)} %bitcast.refs_0_.block_ref, f32[112,16,128]{2,1,0:T(8,128)S(1)} %copy-done.2, f32[112,16,128]{2,1,0:T(8,128)S(1)} %copy-done.3, f32[112,16,128]{2,1,0:T(8,128)S(1)} %collective-permute-done.refs_3_, ...), custom_call_target="tpu_custom_call" | custom-call | flops 35389440 | bytes 4718592 | tf_op jit(solution)/shard_map/two_substeps/pallas_call | solution.py:662
  65.8 0.1 collective-permute-start.4
  65.9 4.0 %collective-permute-start.5 = (f32[54,16,128]{2,1,0:T(8,128)S(1)}, f32[54,16,128]{2,1,0:T(8,128)S(1)}, u32[]{:S(2)}, u32[]{:S(2)}) collective-permute-start(f32[54,16,128]{2,1,0:T(8,128)S(1)} %get-tuple-element.30.refs_2_), channel_id=1, source_target_pairs={{2,4},{4,2},{6,8},{8,6},{10,12},{12,10},{14,16},{16,14},{18,20},{2... | collective-permute-start | bytes 1327112 | tf_op jit(solution)/shard_map/ppermute | solution.py:650
  69.9 0.0 collective-permute-done.6.refs_4_
  69.9 0.0 collective-permute-done.7.refs_5_
  69.9 4.5 %last_substep.2.refs_10_ = f32[1152,512]{1,0:T(8,128)} custom-call(s32[1]{0:T(128)} %bitcast.refs_0_.block_ref, f32[54,16,128]{2,1,0:T(8,128)S(1)} %get-tuple-element.32.refs_1_, f32[54,16,128]{2,1,0:T(8,128)S(1)} %get-tuple-element.33.refs_2_, f32[36,16,128]{2,1,0:T(8,128)S(1)} %get-tuple-element.34.refs_3_, ...), custom_call_target="tpu_custom_call" | custom-call | flops 11796480 | bytes 4718592 | tf_op jit(solution)/shard_map/last_substep/pallas_call | solution.py:686
  74.4 0.0 collective-permute-done.4.refs_4_
  74.5 5.4 %collective-permute-done.5.refs_5_ = f32[54,16,128]{2,1,0:T(8,128)S(1)} collective-permute-done((f32[54,16,128]{2,1,0:T(8,128)S(1)}, f32[54,16,128]{2,1,0:T(8,128)S(1)}, u32[]{:S(2)}, u32[]{:S(2)}) %collective-permute-start.5) | collective-permute-done | bytes 442400 | tf_op jit(solution)/shard_map/ppermute | solution.py:650
  79.9 4.4 %last_substep.3 = f32[1152,512]{1,0:T(8,128)} custom-call(s32[1]{0:T(128)} %bitcast.refs_0_.block_ref, f32[54,16,128]{2,1,0:T(8,128)S(1)} %get-tuple-element.29.refs_1_, f32[54,16,128]{2,1,0:T(8,128)S(1)} %get-tuple-element.30.refs_2_, f32[36,16,128]{2,1,0:T(8,128)S(1)} %get-tuple-element.31.refs_3_, ...), custom_call_target="tpu_custom_call", output_to_operand_aliasing={{}: (10, {})} | custom-call | flops 11796480 | bytes 4718592 | tf_op jit(solution)/shard_map/last_substep/pallas_call | solution.py:686
Async XLA Ops:
  4.6 13.1 %collective-permute-start.2 = (f32[113,16,128]{2,1,0:T(8,128)}, f32[113,16,128]{2,1,0:T(8,128)S(1)}, u32[]{:S(2)}, u32[]{:S(2)}) collective-permute-start(f32[113,16,128]{2,1,0:T(8,128)} %get-tuple-element.22.refs_1_), channel_id=1, source_target_pairs={{0,2},{2,0},{4,6},{6,4},{8,10},{10,8},{12,14},{14,12},{16,18},{18,... | collective-permute-start | bytes 2777096 | tf_op jit(solution)/shard_map/ppermute | solution.py:651
  4.7 35.6 %collective-permute-start.3 = (f32[113,16,128]{2,1,0:T(8,128)}, f32[113,16,128]{2,1,0:T(8,128)S(1)}, u32[]{:S(2)}, u32[]{:S(2)}) collective-permute-start(f32[113,16,128]{2,1,0:T(8,128)} %get-tuple-element.23.refs_2_), channel_id=1, source_target_pairs={{2,4},{4,2},{6,8},{8,6},{10,12},{12,10},{14,16},{16,14},{18,20},{2... | collective-permute-start | bytes 2777096 | tf_op jit(solution)/shard_map/ppermute | solution.py:650
  9.2 32.8 %copy-start = (f32[113,16,128]{2,1,0:T(8,128)S(1)}, f32[113,16,128]{2,1,0:T(8,128)}, u32[]{:S(2)}) copy-start(f32[113,16,128]{2,1,0:T(8,128)} %get-tuple-element.22.refs_1_) | copy-start | bytes 2777092
  9.2 32.8 %copy-start.1 = (f32[113,16,128]{2,1,0:T(8,128)S(1)}, f32[113,16,128]{2,1,0:T(8,128)}, u32[]{:S(2)}) copy-start(f32[113,16,128]{2,1,0:T(8,128)} %get-tuple-element.23.refs_2_) | copy-start | bytes 2777092
  14.0 41.8 %collective-permute-start = (f32[112,16,128]{2,1,0:T(8,128)}, f32[112,16,128]{2,1,0:T(8,128)S(1)}, u32[]{:S(2)}, u32[]{:S(2)}) collective-permute-start(f32[112,16,128]{2,1,0:T(8,128)} %get-tuple-element.20.refs_1_), channel_id=1, source_target_pairs={{0,2},{2,0},{4,6},{6,4},{8,10},{10,8},{12,14},{14,12},{16,18},{18,... | collective-permute-start | bytes 2752520 | tf_op jit(solution)/shard_map/ppermute | solution.py:651
  14.1 41.7 %collective-permute-start.1 = (f32[112,16,128]{2,1,0:T(8,128)}, f32[112,16,128]{2,1,0:T(8,128)S(1)}, u32[]{:S(2)}, u32[]{:S(2)}) collective-permute-start(f32[112,16,128]{2,1,0:T(8,128)} %get-tuple-element.21.refs_2_), channel_id=1, source_target_pairs={{2,4},{4,2},{6,8},{8,6},{10,12},{12,10},{14,16},{16,14},{18,20},{2... | collective-permute-start | bytes 2752520 | tf_op jit(solution)/shard_map/ppermute | solution.py:650
  40.3 0.8 copy-start.4
  42.1 13.8 %copy-start.2 = (f32[112,16,128]{2,1,0:T(8,128)S(1)}, f32[112,16,128]{2,1,0:T(8,128)}, u32[]{:S(2)}) copy-start(f32[112,16,128]{2,1,0:T(8,128)} %get-tuple-element.20.refs_1_) | copy-start | bytes 2752516
  42.1 13.8 %copy-start.3 = (f32[112,16,128]{2,1,0:T(8,128)S(1)}, f32[112,16,128]{2,1,0:T(8,128)}, u32[]{:S(2)}) copy-start(f32[112,16,128]{2,1,0:T(8,128)} %get-tuple-element.21.refs_2_) | copy-start | bytes 2752516
  52.1 17.8 %collective-permute-start.6 = (f32[54,16,128]{2,1,0:T(8,128)S(1)}, f32[54,16,128]{2,1,0:T(8,128)S(1)}, u32[]{:S(2)}, u32[]{:S(2)}) collective-permute-start(f32[54,16,128]{2,1,0:T(8,128)S(1)} %get-tuple-element.32.refs_1_), channel_id=1, source_target_pairs={{0,2},{2,0},{4,6},{6,4},{8,10},{10,8},{12,14},{14,12},{16,18},{18,... | collective-permute-start | bytes 1327112 | tf_op jit(solution)/shard_map/ppermute | solution.py:651
  52.2 17.8 %collective-permute-start.7 = (f32[54,16,128]{2,1,0:T(8,128)S(1)}, f32[54,16,128]{2,1,0:T(8,128)S(1)}, u32[]{:S(2)}, u32[]{:S(2)}) collective-permute-start(f32[54,16,128]{2,1,0:T(8,128)S(1)} %get-tuple-element.33.refs_2_), channel_id=1, source_target_pairs={{2,4},{4,2},{6,8},{8,6},{10,12},{12,10},{14,16},{16,14},{18,20},{2... | collective-permute-start | bytes 1327112 | tf_op jit(solution)/shard_map/ppermute | solution.py:650
  65.8 8.6 %collective-permute-start.4 = (f32[54,16,128]{2,1,0:T(8,128)S(1)}, f32[54,16,128]{2,1,0:T(8,128)S(1)}, u32[]{:S(2)}, u32[]{:S(2)}) collective-permute-start(f32[54,16,128]{2,1,0:T(8,128)S(1)} %get-tuple-element.29.refs_1_), channel_id=1, source_target_pairs={{0,2},{2,0},{4,6},{6,4},{8,10},{10,8},{12,14},{14,12},{16,18},{18,... | collective-permute-start | bytes 1327112 | tf_op jit(solution)/shard_map/ppermute | solution.py:651
  65.9 14.0 %collective-permute-start.5 = (f32[54,16,128]{2,1,0:T(8,128)S(1)}, f32[54,16,128]{2,1,0:T(8,128)S(1)}, u32[]{:S(2)}, u32[]{:S(2)}) collective-permute-start(f32[54,16,128]{2,1,0:T(8,128)S(1)} %get-tuple-element.30.refs_2_), channel_id=1, source_target_pairs={{2,4},{4,2},{6,8},{8,6},{10,12},{12,10},{14,16},{16,14},{18,20},{2... | collective-permute-start | bytes 1327112 | tf_op jit(solution)/shard_map/ppermute | solution.py:650

commit v2 on v1

--- a/solution.py
+++ b/solution.py
@@ -104,7 +104,7 @@
         kit_out = refs.pop(0)
     outs = [refs.pop(0) for _ in range(2)]
     spec, wind_ref, operator, growth_ref, dissipation_ref, rounded, mixed = refs[:7]
-    mask_ref, index_ref, sems = refs[7:10]
+    mask_ref, index_ref, sems, out_sems = refs[7:11]
     span = freqs * ND
     pairs = [(spectrum.at[:, pl.ds(r * LANES, LANES)], spec.at[r]) for r in range(rows)]
     pairs += [
@@ -116,23 +116,28 @@
         (index_in, index_ref),
     ]
     if last:
-        kit = refs[10]
-        depths_ref, speed_ref, refraction_ref = refs[11:]
+        kit = refs[11]
+        depths_ref, speed_ref, refraction_ref = refs[12:]
         pairs += list(zip(tables_in, (depths_ref, speed_ref, refraction_ref)))
     copies = fetch(pairs, sems)
-    for r in range(rows):
-        copies[r].wait()
-        rounded[:, r * LANES : (r + 1) * LANES] = spec[r].astype(jnp.bfloat16)
-    for copy in copies[rows:]:
-        copy.wait()
-    nonlinear = jnp.dot(operator[...], rounded[...], preferred_element_type=jnp.float32)
-    for r in range(rows):
-        mixed[r] = nonlinear[:, r * LANES : (r + 1) * LANES]
     components = spec.shape[1]
-    growth = column_of(growth_ref[...], chunk * freqs, freqs)
-    dissipation = column_of(dissipation_ref[...], chunk * freqs, freqs)
     tiles = freqs // TILE
-    for r in range(rows):
+    odd = lax.rem(block, 2) == 1
+
+    def leave(number, which, start, count):
+        part = pl.ds(start, count)
+
+        def begin(to):
+            pltpu.make_async_copy(outs[which].at[part], to.at[part], out_sems.at[number]).start()
+
+        by_parity(
+            odd,
+            lambda: begin((even_out, odd_out)[which]),
+            lambda: begin((odd_out, even_out)[which]),
+        )
+        return pltpu.make_async_copy(outs[which].at[part], even_out.at[part], out_sems.at[number])
+
+    def work_on(r, growth, dissipation):
         average = jnp.sum(spec[r], axis=0, keepdims=True) * (1.0 / components)
         limited = average / (average + 1.0)
         wind_x = jnp.broadcast_to(wind_ref[0:1, r * LANES : (r + 1) * LANES], (TILE, LANES))
@@ -153,16 +158,38 @@
                 value = energy + (grow[t] * squared - damp[t]) * energy + 0.25 * extra
                 for which, slot in places_two(r, d):
                     outs[which][slot, t * TILE : (t + 1) * TILE, :] = value
+
+    leaving = []
+    growth = dissipation = None
+    for first_row in (0, 2):
+        for r in (first_row, first_row + 1):
+            copies[r].wait()
+            rounded[:, r * LANES : (r + 1) * LANES] = spec[r].astype(jnp.bfloat16)
+        if first_row == 0:
+            for copy in copies[rows:]:
+                copy.wait()
+            growth = column_of(growth_ref[...], chunk * freqs, freqs)
+            dissipation = column_of(dissipation_ref[...], chunk * freqs, freqs)
+        both = slice(first_row * LANES, (first_row + 2) * LANES)
+        nonlinear = jnp.dot(
+            operator[...], rounded[:, both], preferred_element_type=jnp.float32
+        )
+        for r in (first_row, first_row + 1):
+            mixed[r] = nonlinear[:, (r - first_row) * LANES : (r - first_row + 1) * LANES]
+            work_on(r, growth, dissipation)
+        if first_row == 0:
+            leaving += [leave(0, 1, 0, THIRD), leave(1, 0, THIRD, TWO - THIRD)]
+    leaving += [leave(2, 0, 0, THIRD), leave(3, 1, THIRD, TWO - THIRD)]
     first = lax.rem(block, comps) * rows
     mask = mask_ref[...].astype(jnp.float32)
     index = index_ref[...].astype(jnp.float32)
-    leaving = []
     if chunk == 0:
         for out, row in ((outs[0], first + rows - 3), (outs[1], first)):
             for k in range(3):
                 out[TWO, k : k + 1, :] = pick_row(mask, row + k)
                 out[TWO, 3 + k : 4 + k, :] = pick_row(index, row + k)
             out[TWO, 6:, :] = jnp.zeros((freqs - 6, LANES), jnp.float32)
+        leaving += [leave(4, 0, TWO, 1), leave(5, 1, TWO, 1)]
     if last:
         count, levels = speed_ref.shape
         kit[...] = jnp.zeros_like(kit)
@@ -172,12 +199,9 @@
         for r in range(rows):
             kit[2 * count + TILE + r, :] = pick_row(mask, first + r)[0]
             kit[2 * count + TILE + rows + r, :] = pick_row(index, first + r)[0]
-        leaving.append((kit, kit_out))
-    by_parity(
-        lax.rem(block, 2) == 1,
-        lambda: run_copies([(outs[0], even_out), (outs[1], odd_out)] + leaving, sems),
-        lambda: run_copies([(outs[1], even_out), (outs[0], odd_out)] + leaving, sems),
-    )
+        run_copies([(kit, kit_out)], sems)
+    for copy in leaving:
+        copy.wait()
 
 
 def weights(courant):
@@ -251,15 +275,18 @@
 
 
 def shift_rows_columns(
-    part, first, last, cells_of, moved, x_ref, y_ref, base, trig, j, members, put
+    part, first, last, cells_of, moved, x_ref, y_ref, base, trig, j, members, rows_of
 ):
+    count = last - first + 1
+    faces_x = x_ref.at[pl.ds(base + first, count + 1), part]
+    faces_y = y_ref.at[pl.ds(base + first, count), part]
     along_x = {
-        k: weights(x_ref[base + k, part, :] * trig[0, j]) for k in range(first, last + 2)
+        k: weights(faces_x[k - first] * trig[0, j]) for k in range(first, last + 2)
     }
     for i, (d, _, up, _) in enumerate(members):
-        cell = functools.partial(cells_of, d)
+        cell = cells_of(d)
         if up:
-            cells = {r: cell(r) for r in range(first - 2, last + 2)}
+            cells = {r: cell[r - first + 2] for r in range(first - 2, last + 2)}
             faces = {
                 k: a * cells[k - 1] + b * cells[k] - c * cells[k - 2]
                 for k, (a, b, c) in along_x.items()
@@ -267,7 +294,7 @@
             for r in range(first, last + 1):
                 moved[i, r - first] = cells[r] - (faces[r + 1] - faces[r])
         else:
-            cells = {r: cell(r) for r in range(first - 1, last + 3)}
+            cells = {r: cell[r - first + 2] for r in range(first - 1, last + 3)}
             faces = {
                 k: a * cells[k] + b * cells[k - 1] - c * cells[k + 1]
                 for k, (a, b, c) in along_x.items()
@@ -277,11 +304,12 @@
     lanes = lax.broadcasted_iota(jnp.int32, (TILE, LANES), 1)
     not_first = (lanes != 0).astype(jnp.float32)
     not_last = (lanes != LANES - 2).astype(jnp.float32)
+    results = [rows_of(d) for _, d, _, _ in members]
     for r in range(first, last + 1):
-        near, far, curve = weights(y_ref[base + r, part, :] * trig[1, j])
+        near, far, curve = weights(faces_y[r - first] * trig[1, j])
         curve_up = curve * not_first
         curve_down = curve * not_last
-        for i, (_, d, _, to_higher) in enumerate(members):
+        for i, (_, _, _, to_higher) in enumerate(members):
             here = moved[i, r - first]
             after = pltpu.roll(here, LANES - 1, 1)
             if to_higher:
@@ -292,7 +320,7 @@
                 beyond = pltpu.roll(here, LANES - 2, 1)
                 face = near * after + far * here - curve_down * beyond
                 result = here + (face - pltpu.roll(face, 1, 1))
-            put(r, d, result)
+            results[i][r - first] = result
 
 
 def every_class(tiles, one_class):
@@ -310,14 +338,14 @@
             one_class(t, j, members)
 
 
-def turn_rows(jobs):
+def turn_row(cells, turnings, land, out):
     half_turn = ND // 2
 
-    def slope(read, i):
-        return read((i + 1) % ND) - read(i % ND)
-
-    def pair(read, turning, d, known):
-        courant = turning(d)
+    def slope(i):
+        return cells[(i + 1) % ND] - cells[i % ND]
+
+    def pair(d, known):
+        courant = turnings[d]
         half = 0.5 * courant
         spread = (1.0 / 3.0) - courant * (courant * (1.0 / 3.0))
         positive = courant >= 0.0
@@ -326,9 +354,9 @@
         for side in range(2):
             own = d + side * half_turn
             rise, bend = known[side]
-            next_rise = slope(read, own + 1)
+            next_rise = slope(own + 1)
             next_bend = next_rise - rise
-            total = read(own) + read((own + 1) % ND)
+            total = cells[own] + cells[(own + 1) % ND]
             if side == 0:
                 chosen = jnp.where(positive, bend, next_bend)
                 faces.append(half * ((total - courant * rise) - spread * chosen))
@@ -338,29 +366,23 @@
             following.append((next_rise, next_bend))
         return faces, following
 
-    def known_at(read, d):
-        found = []
-        for side in range(2):
-            own = d + side * half_turn
-            rise = slope(read, own)
-            found.append((rise, rise - slope(read, own - 1)))
-        return found
-
-    states = []
-    for read, turning, _, _ in jobs:
-        ends, following = pair(read, turning, half_turn - 1, known_at(read, half_turn - 1))
-        states.append((ends, [0.0 - ends[1], 0.0 - ends[0]], [following[1], following[0]]))
+    known = []
+    for side in range(2):
+        own = half_turn - 1 + side * half_turn
+        rise = slope(own)
+        known.append((rise, rise - slope(own - 1)))
+    ends, following = pair(half_turn - 1, known)
+    previous = [0.0 - ends[1], 0.0 - ends[0]]
+    known = [following[1], following[0]]
     for d in range(half_turn):
-        for i, (read, turning, land, put) in enumerate(jobs):
-            ends, previous, known = states[i]
-            if d == half_turn - 1:
-                current = ends
-            else:
-                current, known = pair(read, turning, d, known)
-            put(d, (read(d) - (current[0] - previous[0])) * land)
-            own = d + half_turn
-            put(own, (read(own) + (current[1] - previous[1])) * land)
-            states[i] = (ends, current, known)
+        if d == half_turn - 1:
+            current = ends
+        else:
+            current, known = pair(d, known)
+        out[d] = (cells[d] - (current[0] - previous[0])) * land
+        own = d + half_turn
+        out[own] = (cells[own] + (current[1] - previous[1])) * land
+        previous = current
 
 
 def set_trig(trig):
@@ -413,11 +435,11 @@
         base = jnp.where(stage == 0, 2, jnp.where(stage == 1, 6, 4))
 
         def one_class(t, j, members):
-            def cell(d, r):
-                return cells[source, t, base + r, d]
-
-            def put(r, d, value):
-                work[t, r, d] = value
+            def cell(d):
+                return cells.at[source, t, pl.ds(base - 2, 8), d]
+
+            def put(d):
+                return work.at[t, :, d]
 
             table = pl.ds(chunk * freqs + t * TILE, TILE)
             shift_rows_columns(
@@ -430,19 +452,12 @@
         def _(i):
             t = i // 4
             r = lax.rem(i, 4)
-
-            def put(d, value):
-                cells[1 - source, t, base + r, d] = value
-
-            turn_rows(
-                [
-                    (
-                        lambda d: work[t, r, d],
-                        lambda d: turn_ref[chunk * tiles + t, (base - 2 + r) * half_turn + d],
-                        land_ref[base - 2 + r],
-                        put,
-                    )
-                ]
+            turning = pl.ds((base - 2 + r) * half_turn, half_turn)
+            turn_row(
+                work.at[t, r],
+                turn_ref.at[chunk * tiles + t, turning],
+                land_ref[base - 2 + r],
+                cells.at[1 - source, t, base + r],
             )
 
     def hand_out(up_out, down_out):
@@ -506,11 +521,11 @@
     )
 
     def only_pass(t, j, members):
-        def cell(d, r):
-            return cells[t, r + 2, d]
-
-        def put(r, d, value):
-            work[t, r, d] = value
+        def cell(d):
+            return cells.at[t, :, d]
+
+        def put(d):
+            return work.at[t, :, d]
 
         table = pl.ds(chunk * freqs + t * TILE, TILE)
         shift_rows_columns(
@@ -524,19 +539,19 @@
         t = i // 4
         r = lax.rem(i, 4)
 
-        def put(d, value):
-            packed[r, pl.ds(t * (TILE * ND) + d, TILE, stride=ND), :] = value
-
-        turn_rows(
-            [
-                (
-                    lambda d: work[t, r, d],
-                    lambda d: turn_ref[chunk * tiles + t, (r + 2) * half_turn + d],
-                    land_ref[r + 2],
-                    put,
-                )
-            ]
+        turn_row(
+            work.at[t, r],
+            turn_ref.at[chunk * tiles + t, pl.ds((r + 2) * half_turn, half_turn)],
+            land_ref[r + 2],
+            cells.at[t, r + 2],
         )
+
+    @pl.loop(0, ND)
+    def _(d):
+        for t in range(tiles):
+            for r in range(rows):
+                place = pl.ds(t * (TILE * ND) + d, TILE, stride=ND)
+                packed[r, place, :] = cells[t, r + 2, d]
 
     run_copies(
         [
@@ -611,6 +626,7 @@
             like(sea_mask),
             like(depth_index),
             pltpu.SemaphoreType.DMA((14,)),
+            pltpu.SemaphoreType.DMA((6,)),
         ]
         if last:
             shapes.append(block(2 * nfreq + 2 * TILE, LANES))

time: 84.7 us -> 85.5 us (level)
  Pallas kernels: 39.2 us -> 40.9 us
  waiting for transfers between devices: 28.1 us -> 27.2 us
    pallas_call x2, Pallas kernels: 9.4 us -> 10.6 us  [source(): pl.pallas_call(functools.partial(source_kernel, chunk, freqs, last, comps...]
    ppermute x4, waiting for transfers between devices: 28.1 us -> 27.2 us  [exchange(): odd = lax.ppermute(odd, BLOCKS, odd_swaps)]
where the time goes in v2:
time: 85.5 us; the launch traced here: 85.2 us
  Pallas kernels  40.9 us (48%)
  waiting for transfers between devices  27.2 us (32%)
  starting transfers between devices  16 us (19%)
    ppermute x4, waiting for transfers between devices, exchange(): odd = lax.ppermute(odd, BLOCKS, odd_swaps)  27.2 us
    pallas_call x2, Pallas kernels, two_steps(): pl.pallas_call(functools.partial(two_steps_kernel, chunk, freqs), in_spec...  19.9 us
    ppermute x4, starting transfers between devices, exchange(): odd = lax.ppermute(odd, BLOCKS, odd_swaps)  15.7 us
    pallas_call x2, Pallas kernels, source(): pl.pallas_call(functools.partial(source_kernel, chunk, freqs, last, comps...  10.6 us
    pallas_call x2, Pallas kernels, last_step(): pl.pallas_call(functools.partial(last_step_kernel, chunk, freqs), in_spec...  9.54 us
  transfers between devices with their start and end apart: 8, of which 2 were waited for; matrix products, arithmetic and copies ran while one was open for 0% of the time, Pallas kernels for 36%

profile of v2, /device:TPU:1, one launch (start us, length us, event | category | flops | bytes accessed | tf_op | source)
XLA Modules:
  0.0 85.2 jit_solution(5828417781133118458)
XLA Ops:
  0.0 5.2 %source_terms.3 = (f32[113,16,128]{2,1,0:T(8,128)}, f32[113,16,128]{2,1,0:T(8,128)}) custom-call(s32[1]{0:T(128)} %bitcast.refs_0_.block_ref, f32[1152,512]{1,0:T(8,128)} %refs_1_.3, f32[2,512]{1,0:T(2,128)} %refs_2_.3, bf16[1152,1152]{1,0:T(8,128)(2,1)} %refs_3_.3, f32[1,32]{1,0:T(1,128)} %bitcast.4, f32[1,32]{1,0:T(1,128)} %bitcast.6, s32[64,128]{1,0:T(8,128)} %refs_6_.3, ...), custom_call_target="tpu_custom_call" | custom-call | flops 679477248 | bytes 2359296 | tf_op jit(solution)/shard_map/source_terms/pallas_call | solution.py:636
  5.2 0.1 collective-permute-start.2
  5.3 4.5 %collective-permute-start.3 = (f32[113,16,128]{2,1,0:T(8,128)}, f32[113,16,128]{2,1,0:T(8,128)S(1)}, u32[]{:S(2)}, u32[]{:S(2)}) collective-permute-start(f32[113,16,128]{2,1,0:T(8,128)} %get-tuple-element.23.refs_2_), channel_id=1, source_target_pairs={{2,4},{4,2},{6,8},{8,6},{10,12},{12,10},{14,16},{16,14},{18,20},{2... | collective-permute-start | bytes 2777096 | tf_op jit(solution)/shard_map/ppermute | solution.py:666
  9.8 0.0 copy-start
  9.8 0.0 copy-start.1
  9.8 5.4 %source_terms.2 = (f32[112,16,128]{2,1,0:T(8,128)}, f32[112,16,128]{2,1,0:T(8,128)}, f32[80,128]{1,0:T(8,128)}) custom-call(s32[1]{0:T(128)} %bitcast.refs_0_.block_ref, f32[1152,512]{1,0:T(8,128)} %refs_1_.3, f32[2,512]{1,0:T(2,128)} %refs_2_.3, bf16[1152,1152]{1,0:T(8,128)(2,1)} %refs_3_.3, f32[1,32]{1,0:T(1,128)} %bitcast.5, f32[1,32]{1,0:T(1,128)} %bitcast.7, ...), custom_call_target="tpu_custom_call" | custom-call | flops 679477248 | bytes 2359296 | tf_op jit(solution)/shard_map/source_terms/pallas_call | solution.py:636
  15.2 0.1 collective-permute-start
  15.3 3.5 %collective-permute-start.1 = (f32[112,16,128]{2,1,0:T(8,128)}, f32[112,16,128]{2,1,0:T(8,128)S(1)}, u32[]{:S(2)}, u32[]{:S(2)}) collective-permute-start(f32[112,16,128]{2,1,0:T(8,128)} %get-tuple-element.21.refs_2_), channel_id=1, source_target_pairs={{2,4},{4,2},{6,8},{8,6},{10,12},{12,10},{14,16},{16,14},{18,20},{2... | collective-permute-start | bytes 2752520 | tf_op jit(solution)/shard_map/ppermute | solution.py:666
  18.8 0.0 collective-permute-done.2.even_ref.refs_3_
  18.8 22.1 %collective-permute-done.3.odd_ref.refs_4_ = f32[113,16,128]{2,1,0:T(8,128)S(1)} collective-permute-done((f32[113,16,128]{2,1,0:T(8,128)}, f32[113,16,128]{2,1,0:T(8,128)S(1)}, u32[]{:S(2)}, u32[]{:S(2)}) %collective-permute-start.3) | collective-permute-done | bytes 925728 | tf_op jit(solution)/shard_map/ppermute | solution.py:666
  40.9 0.0 copy-start.4
  40.9 0.8 copy-done.4
  41.7 0.9 %coast_tables.1 = (f32[9,32,128]{2,1,0:T(8,128)S(1)}, f32[8,32,128]{2,1,0:T(8,128)S(1)}, f32[4,144,8,128]{3,2,1,0:T(8,128)S(1)}, f32[8,8,128]{2,1,0:T(8,128)S(1)}) custom-call(s32[1]{0:T(128)} %bitcast.refs_0_.block_ref, f32[113,16,128]{2,1,0:T(8,128)S(1)} %collective-permute-done.2.even_ref.refs_3_, ...), custom_call_target="tpu_custom_call" | custom-call | flops 589824 | bytes 2359296 | tf_op jit(solution)/shard_map/coast_tables/pallas_call | solution.py:654
  42.6 0.0 copy-done
  42.6 0.0 copy-done.1
  42.6 0.0 copy-start.2
  42.7 0.0 copy-start.3
  42.7 10.0 %two_substeps.3 = (f32[54,16,128]{2,1,0:T(8,128)S(1)}, f32[54,16,128]{2,1,0:T(8,128)S(1)}, f32[36,16,128]{2,1,0:T(8,128)S(1)}) custom-call(s32[1]{0:T(128)} %bitcast.refs_0_.block_ref, f32[113,16,128]{2,1,0:T(8,128)S(1)} %copy-done, f32[113,16,128]{2,1,0:T(8,128)S(1)} %copy-done.1, f32[113,16,128]{2,1,0:T(8,128)S(1)} %collective-permute-done.2.even_ref.refs_3_, ...), custom_call_target="tpu_custom_call" | custom-call | flops 35389440 | bytes 4718592 | tf_op jit(solution)/shard_map/two_substeps/pallas_call | solution.py:678
  52.6 0.1 collective-permute-start.6
  52.7 3.6 %collective-permute-start.7 = (f32[54,16,128]{2,1,0:T(8,128)S(1)}, f32[54,16,128]{2,1,0:T(8,128)S(1)}, u32[]{:S(2)}, u32[]{:S(2)}) collective-permute-start(f32[54,16,128]{2,1,0:T(8,128)S(1)} %get-tuple-element.33.refs_2_), channel_id=1, source_target_pairs={{2,4},{4,2},{6,8},{8,6},{10,12},{12,10},{14,16},{16,14},{18,20},{2... | collective-permute-start | bytes 1327112 | tf_op jit(solution)/shard_map/ppermute | solution.py:666
  56.4 0.0 collective-permute-done.refs_3_
  56.4 0.0 collective-permute-done.1.refs_4_
  56.4 0.0 copy-done.2
  56.4 0.0 copy-done.3
  56.4 10.0 %two_substeps.2 = (f32[54,16,128]{2,1,0:T(8,128)S(1)}, f32[54,16,128]{2,1,0:T(8,128)S(1)}, f32[36,16,128]{2,1,0:T(8,128)S(1)}) custom-call(s32[1]{0:T(128)} %bitcast.refs_0_.block_ref, f32[112,16,128]{2,1,0:T(8,128)S(1)} %copy-done.2, f32[112,16,128]{2,1,0:T(8,128)S(1)} %copy-done.3, f32[112,16,128]{2,1,0:T(8,128)S(1)} %collective-permute-done.refs_3_, ...), custom_call_target="tpu_custom_call" | custom-call | flops 35389440 | bytes 4718592 | tf_op jit(solution)/shard_map/two_substeps/pallas_call | solution.py:678
  66.4 0.1 collective-permute-start.4
  66.5 4.0 %collective-permute-start.5 = (f32[54,16,128]{2,1,0:T(8,128)S(1)}, f32[54,16,128]{2,1,0:T(8,128)S(1)}, u32[]{:S(2)}, u32[]{:S(2)}) collective-permute-start(f32[54,16,128]{2,1,0:T(8,128)S(1)} %get-tuple-element.30.refs_2_), channel_id=1, source_target_pairs={{2,4},{4,2},{6,8},{8,6},{10,12},{12,10},{14,16},{16,14},{18,20},{2... | collective-permute-start | bytes 1327112 | tf_op jit(solution)/shard_map/ppermute | solution.py:666
  70.5 0.0 collective-permute-done.6.refs_4_
  70.5 0.0 collective-permute-done.7.refs_5_
  70.5 4.8 %last_substep.2.refs_10_ = f32[1152,512]{1,0:T(8,128)} custom-call(s32[1]{0:T(128)} %bitcast.refs_0_.block_ref, f32[54,16,128]{2,1,0:T(8,128)S(1)} %get-tuple-element.32.refs_1_, f32[54,16,128]{2,1,0:T(8,128)S(1)} %get-tuple-element.33.refs_2_, f32[36,16,128]{2,1,0:T(8,128)S(1)} %get-tuple-element.34.refs_3_, ...), custom_call_target="tpu_custom_call" | custom-call | flops 11796480 | bytes 4718592 | tf_op jit(solution)/shard_map/last_substep/pallas_call | solution.py:702
  75.3 0.0 collective-permute-done.4.refs_4_
  75.3 5.1 %collective-permute-done.5.refs_5_ = f32[54,16,128]{2,1,0:T(8,128)S(1)} collective-permute-done((f32[54,16,128]{2,1,0:T(8,128)S(1)}, f32[54,16,128]{2,1,0:T(8,128)S(1)}, u32[]{:S(2)}, u32[]{:S(2)}) %collective-permute-start.5) | collective-permute-done | bytes 442400 | tf_op jit(solution)/shard_map/ppermute | solution.py:666
  80.4 4.7 %last_substep.3 = f32[1152,512]{1,0:T(8,128)} custom-call(s32[1]{0:T(128)} %bitcast.refs_0_.block_ref, f32[54,16,128]{2,1,0:T(8,128)S(1)} %get-tuple-element.29.refs_1_, f32[54,16,128]{2,1,0:T(8,128)S(1)} %get-tuple-element.30.refs_2_, f32[36,16,128]{2,1,0:T(8,128)S(1)} %get-tuple-element.31.refs_3_, ...), custom_call_target="tpu_custom_call", output_to_operand_aliasing={{}: (10, {})} | custom-call | flops 11796480 | bytes 4718592 | tf_op jit(solution)/shard_map/last_substep/pallas_call | solution.py:702
Async XLA Ops:
  5.2 13.6 %collective-permute-start.2 = (f32[113,16,128]{2,1,0:T(8,128)}, f32[113,16,128]{2,1,0:T(8,128)S(1)}, u32[]{:S(2)}, u32[]{:S(2)}) collective-permute-start(f32[113,16,128]{2,1,0:T(8,128)} %get-tuple-element.22.refs_1_), channel_id=1, source_target_pairs={{0,2},{2,0},{4,6},{6,4},{8,10},{10,8},{12,14},{14,12},{16,18},{18,... | collective-permute-start | bytes 2777096 | tf_op jit(solution)/shard_map/ppermute | solution.py:667
  5.3 35.6 %collective-permute-start.3 = (f32[113,16,128]{2,1,0:T(8,128)}, f32[113,16,128]{2,1,0:T(8,128)S(1)}, u32[]{:S(2)}, u32[]{:S(2)}) collective-permute-start(f32[113,16,128]{2,1,0:T(8,128)} %get-tuple-element.23.refs_2_), channel_id=1, source_target_pairs={{2,4},{4,2},{6,8},{8,6},{10,12},{12,10},{14,16},{16,14},{18,20},{2... | collective-permute-start | bytes 2777096 | tf_op jit(solution)/shard_map/ppermute | solution.py:666
  9.8 32.8 %copy-start = (f32[113,16,128]{2,1,0:T(8,128)S(1)}, f32[113,16,128]{2,1,0:T(8,128)}, u32[]{:S(2)}) copy-start(f32[113,16,128]{2,1,0:T(8,128)} %get-tuple-element.22.refs_1_) | copy-start | bytes 2777092
  9.8 32.8 %copy-start.1 = (f32[113,16,128]{2,1,0:T(8,128)S(1)}, f32[113,16,128]{2,1,0:T(8,128)}, u32[]{:S(2)}) copy-start(f32[113,16,128]{2,1,0:T(8,128)} %get-tuple-element.23.refs_2_) | copy-start | bytes 2777092
  15.2 41.2 %collective-permute-start = (f32[112,16,128]{2,1,0:T(8,128)}, f32[112,16,128]{2,1,0:T(8,128)S(1)}, u32[]{:S(2)}, u32[]{:S(2)}) collective-permute-start(f32[112,16,128]{2,1,0:T(8,128)} %get-tuple-element.20.refs_1_), channel_id=1, source_target_pairs={{0,2},{2,0},{4,6},{6,4},{8,10},{10,8},{12,14},{14,12},{16,18},{18,... | collective-permute-start | bytes 2752520 | tf_op jit(solution)/shard_map/ppermute | solution.py:667
  15.3 41.1 %collective-permute-start.1 = (f32[112,16,128]{2,1,0:T(8,128)}, f32[112,16,128]{2,1,0:T(8,128)S(1)}, u32[]{:S(2)}, u32[]{:S(2)}) collective-permute-start(f32[112,16,128]{2,1,0:T(8,128)} %get-tuple-element.21.refs_2_), channel_id=1, source_target_pairs={{2,4},{4,2},{6,8},{8,6},{10,12},{12,10},{14,16},{16,14},{18,20},{2... | collective-permute-start | bytes 2752520 | tf_op jit(solution)/shard_map/ppermute | solution.py:666
  40.9 0.8 copy-start.4
  42.6 13.7 %copy-start.2 = (f32[112,16,128]{2,1,0:T(8,128)S(1)}, f32[112,16,128]{2,1,0:T(8,128)}, u32[]{:S(2)}) copy-start(f32[112,16,128]{2,1,0:T(8,128)} %get-tuple-element.20.refs_1_) | copy-start | bytes 2752516
  42.7 13.7 %copy-start.3 = (f32[112,16,128]{2,1,0:T(8,128)S(1)}, f32[112,16,128]{2,1,0:T(8,128)}, u32[]{:S(2)}) copy-start(f32[112,16,128]{2,1,0:T(8,128)} %get-tuple-element.21.refs_2_) | copy-start | bytes 2752516
  52.6 17.8 %collective-permute-start.6 = (f32[54,16,128]{2,1,0:T(8,128)S(1)}, f32[54,16,128]{2,1,0:T(8,128)S(1)}, u32[]{:S(2)}, u32[]{:S(2)}) collective-permute-start(f32[54,16,128]{2,1,0:T(8,128)S(1)} %get-tuple-element.32.refs_1_), channel_id=1, source_target_pairs={{0,2},{2,0},{4,6},{6,4},{8,10},{10,8},{12,14},{14,12},{16,18},{18,... | collective-permute-start | bytes 1327112 | tf_op jit(solution)/shard_map/ppermute | solution.py:667
  52.7 17.8 %collective-permute-start.7 = (f32[54,16,128]{2,1,0:T(8,128)S(1)}, f32[54,16,128]{2,1,0:T(8,128)S(1)}, u32[]{:S(2)}, u32[]{:S(2)}) collective-permute-start(f32[54,16,128]{2,1,0:T(8,128)S(1)} %get-tuple-element.33.refs_2_), channel_id=1, source_target_pairs={{2,4},{4,2},{6,8},{8,6},{10,12},{12,10},{14,16},{16,14},{18,20},{2... | collective-permute-start | bytes 1327112 | tf_op jit(solution)/shard_map/ppermute | solution.py:666
  66.4 8.9 %collective-permute-start.4 = (f32[54,16,128]{2,1,0:T(8,128)S(1)}, f32[54,16,128]{2,1,0:T(8,128)S(1)}, u32[]{:S(2)}, u32[]{:S(2)}) collective-permute-start(f32[54,16,128]{2,1,0:T(8,128)S(1)} %get-tuple-element.29.refs_1_), channel_id=1, source_target_pairs={{0,2},{2,0},{4,6},{6,4},{8,10},{10,8},{12,14},{14,12},{16,18},{18,... | collective-permute-start | bytes 1327112 | tf_op jit(solution)/shard_map/ppermute | solution.py:667
  66.5 14.0 %collective-permute-start.5 = (f32[54,16,128]{2,1,0:T(8,128)S(1)}, f32[54,16,128]{2,1,0:T(8,128)S(1)}, u32[]{:S(2)}, u32[]{:S(2)}) collective-permute-start(f32[54,16,128]{2,1,0:T(8,128)S(1)} %get-tuple-element.30.refs_2_), channel_id=1, source_target_pairs={{2,4},{4,2},{6,8},{8,6},{10,12},{12,10},{14,16},{16,14},{18,20},{2... | collective-permute-start | bytes 1327112 | tf_op jit(solution)/shard_map/ppermute | solution.py:666

commit v3 on v1

--- a/solution.py
+++ b/solution.py
@@ -12,6 +12,7 @@
 LANES = 128
 TILE = 8
 CHUNKS = 2
+WIDE_FIRST = (False, True)
 BLOCKS = ("comp", "space")
 
 ANGLES = 2.0 * np.pi * np.arange(ND) / ND
@@ -90,21 +91,21 @@
     pl.when(odd)(odd_way)
 
 
-def source_kernel(chunk, freqs, last, comps, *refs):
+def source_kernel(chunk, freqs, wide, last, comps, *refs):
     refs = list(refs)
     rows = 4
     block = refs.pop(0)[0]
-    spectrum, wind, coupling, growth_in, dissipation_in, mask_in, index_in = (
-        refs.pop(0) for _ in range(7)
-    )
+    spectrum, wind, coupling, growth_in, dissipation_in = (refs.pop(0) for _ in range(5))
     if last:
-        tables_in = [refs.pop(0) for _ in range(3)]
+        coast_in = [refs.pop(0) for _ in range(5)]
     even_out, odd_out = refs.pop(0), refs.pop(0)
+    if not wide:
+        rest_out = refs.pop(0)
     if last:
-        kit_out = refs.pop(0)
-    outs = [refs.pop(0) for _ in range(2)]
+        kit, edge = refs.pop(0), refs.pop(0)
+    outs = [refs.pop(0) for _ in range(2 if wide else 3)]
     spec, wind_ref, operator, growth_ref, dissipation_ref, rounded, mixed = refs[:7]
-    mask_ref, index_ref, sems = refs[7:10]
+    sems, out_sems = refs[7:9]
     span = freqs * ND
     pairs = [(spectrum.at[:, pl.ds(r * LANES, LANES)], spec.at[r]) for r in range(rows)]
     pairs += [
@@ -112,13 +113,10 @@
         (wind, wind_ref),
         (growth_in, growth_ref),
         (dissipation_in, dissipation_ref),
-        (mask_in, mask_ref),
-        (index_in, index_ref),
     ]
     if last:
-        kit = refs[10]
-        depths_ref, speed_ref, refraction_ref = refs[11:]
-        pairs += list(zip(tables_in, (depths_ref, speed_ref, refraction_ref)))
+        mask_ref, index_ref, depths_ref, speed_ref, refraction_ref = refs[9:]
+        pairs += list(zip(coast_in, refs[9:]))
     copies = fetch(pairs, sems)
     for r in range(rows):
         copies[r].wait()
@@ -132,7 +130,22 @@
     growth = column_of(growth_ref[...], chunk * freqs, freqs)
     dissipation = column_of(dissipation_ref[...], chunk * freqs, freqs)
     tiles = freqs // TILE
-    for r in range(rows):
+    odd = lax.rem(block, 2) == 1
+
+    def leave(number, which, start, count):
+        part = pl.ds(start, count)
+
+        def begin(to):
+            pltpu.make_async_copy(outs[which].at[part], to.at[part], out_sems.at[number]).start()
+
+        by_parity(
+            odd,
+            lambda: begin((even_out, odd_out)[which]),
+            lambda: begin((odd_out, even_out)[which]),
+        )
+        return pltpu.make_async_copy(outs[which].at[part], even_out.at[part], out_sems.at[number])
+
+    for r in (3, 2, 1, 0):
         average = jnp.sum(spec[r], axis=0, keepdims=True) * (1.0 / components)
         limited = average / (average + 1.0)
         wind_x = jnp.broadcast_to(wind_ref[0:1, r * LANES : (r + 1) * LANES], (TILE, LANES))
@@ -151,33 +164,37 @@
                 energy = spec[r, pl.ds(base, TILE, stride=ND), :]
                 extra = mixed[r, pl.ds(t * TILE * ND + d, TILE, stride=ND), :]
                 value = energy + (grow[t] * squared - damp[t]) * energy + 0.25 * extra
-                for which, slot in places_two(r, d):
+                for which, slot in (places_two if wide else places_one)(r, d):
                     outs[which][slot, t * TILE : (t + 1) * TILE, :] = value
-    first = lax.rem(block, comps) * rows
-    mask = mask_ref[...].astype(jnp.float32)
-    index = index_ref[...].astype(jnp.float32)
-    leaving = []
-    if chunk == 0:
-        for out, row in ((outs[0], first + rows - 3), (outs[1], first)):
-            for k in range(3):
-                out[TWO, k : k + 1, :] = pick_row(mask, row + k)
-                out[TWO, 3 + k : 4 + k, :] = pick_row(index, row + k)
-            out[TWO, 6:, :] = jnp.zeros((freqs - 6, LANES), jnp.float32)
+        if r == 2 and wide:
+            leaving = [leave(0, 0, 0, THIRD), leave(1, 1, THIRD, TWO - THIRD)]
+        elif r == 2:
+            leaving = [leave(0, 0, 0, ONE)]
+    if wide:
+        leaving += [leave(2, 1, 0, THIRD), leave(3, 0, THIRD, TWO - THIRD)]
+    else:
+        rest_copy = pltpu.make_async_copy(outs[2], rest_out, out_sems.at[2])
+        rest_copy.start()
+        leaving += [leave(1, 1, 0, ONE), rest_copy]
     if last:
+        first = lax.rem(block, comps) * rows
+        mask = mask_ref[...].astype(jnp.float32)
+        index = index_ref[...].astype(jnp.float32)
         count, levels = speed_ref.shape
         kit[...] = jnp.zeros_like(kit)
         kit[:count, :levels] = speed_ref[...]
         kit[count : 2 * count, :levels] = refraction_ref[...]
         kit[2 * count : 2 * count + 1, :levels] = depths_ref[...]
-        for r in range(rows):
-            kit[2 * count + TILE + r, :] = pick_row(mask, first + r)[0]
-            kit[2 * count + TILE + rows + r, :] = pick_row(index, first + r)[0]
-        leaving.append((kit, kit_out))
-    by_parity(
-        lax.rem(block, 2) == 1,
-        lambda: run_copies([(outs[0], even_out), (outs[1], odd_out)] + leaving, sems),
-        lambda: run_copies([(outs[1], even_out), (outs[0], odd_out)] + leaving, sems),
-    )
+        for k in range(rows + 6):
+            kit[2 * count + TILE + k, :] = pick_row(mask, first + k - 3)[0]
+            kit[2 * count + 3 * TILE + k, :] = pick_row(index, first + k - 3)[0]
+        near_side = first + jnp.where(odd, rows - 3, 0)
+        edge[...] = jnp.zeros_like(edge)
+        for k in range(3):
+            edge[k, :] = pick_row(mask, near_side + k)[0]
+            edge[3 + k, :] = pick_row(index, near_side + k)[0]
+    for copy in leaving:
+        copy.wait()
 
 
 def weights(courant):
@@ -190,21 +207,22 @@
 
 
 def coast_kernel(
-    count, block_ref, even_ref, odd_ref, kit_ref, face_x, face_y, turn_ref, land_ref, slope_by
+    count, block_ref, far_ref, kit_ref, face_x, face_y, turn_ref, land_ref, slope_by
 ):
     rows = 4
     tables = kit_ref[: 2 * count + TILE, :]
-    odd = lax.rem(block_ref[0], 2) == 1
-    even, odds = even_ref[TWO, :TILE, :], odd_ref[TWO, :TILE, :]
-    low, high = jnp.where(odd, even, odds), jnp.where(odd, odds, even)
-    masks = [low[k : k + 1] for k in range(3)]
-    levels = [low[3 + k : 4 + k] for k in range(3)]
-    for r in range(rows):
-        row = 2 * count + TILE + r
-        masks.append(kit_ref[row : row + 1, :])
-        levels.append(kit_ref[row + rows : row + rows + 1, :])
-    masks += [high[k : k + 1] for k in range(3)]
-    levels += [high[3 + k : 4 + k] for k in range(3)]
+    odd = (lax.rem(block_ref[0], 2) == 1).astype(jnp.float32)
+
+    def with_far(start, part):
+        found = [kit_ref[start + k : start + k + 1, :] for k in range(rows + 6)]
+        for k in range(3):
+            far = far_ref[part + k : part + k + 1, :]
+            found[k] += far * (1.0 - odd)
+            found[rows + 3 + k] += far * odd
+        return found
+
+    masks = with_far(2 * count + TILE, 0)
+    levels = with_far(2 * count + 3 * TILE, 3)
     wanted = jnp.concatenate(levels, axis=1)
     entry = lax.broadcasted_iota(jnp.int32, (LANES, wanted.shape[1]), 0).astype(jnp.float32)
     onehot = (entry == wanted).astype(jnp.float32)
@@ -369,10 +387,17 @@
         trig[1, j] = abs(SIN[j])
 
 
-def two_steps_kernel(chunk, freqs, *refs):
+def output_row(packed, out_ref, start, span, r, sems):
+    lanes = pl.ds(pl.multiple_of(r * LANES, LANES), LANES)
+    return pltpu.make_async_copy(packed.at[r], out_ref.at[pl.ds(start, span), lanes], sems.at[r])
+
+
+def two_steps_kernel(chunk, freqs, final, *refs):
     block_ref, even_own, odd_own, even_ref, odd_ref, x_ref, y_ref, turn_ref, land_ref = refs[:9]
-    even_out, odd_out, rest_out = refs[9:12]
-    cells, work, moved, trig = refs[12:]
+    if final:
+        out_ref, cells, work, moved, trig, packed, sems = refs[-7:]
+    else:
+        even_out, odd_out, rest_out, cells, work, moved, trig = refs[-7:]
     odd = lax.rem(block_ref[0], 2) == 1
     tiles = freqs // TILE
     half_turn = ND // 2
@@ -445,6 +470,24 @@
                 ]
             )
 
+    if final:
+        span = freqs * ND
+        rows = 4
+
+        @pl.loop(0, rows)
+        def _(r):
+            @pl.loop(0, ND)
+            def _(d):
+                for t in range(tiles):
+                    place = pl.ds(t * (TILE * ND) + d, TILE, stride=ND)
+                    packed[r, place, :] = cells[0, t, rows + r, d]
+
+            output_row(packed, out_ref, chunk * span, span, r, sems).start()
+
+        for r in range(rows):
+            output_row(packed, out_ref, chunk * span, span, r, sems).wait()
+        return
+
     def hand_out(up_out, down_out):
         @pl.loop(0, ND)
         def _(d):
@@ -464,14 +507,15 @@
     by_parity(odd, lambda: hand_out(even_out, odd_out), lambda: hand_out(odd_out, even_out))
 
 
-def last_step_kernel(chunk, freqs, *refs):
+def one_step_kernel(chunk, freqs, final, *refs):
     refs = list(refs)
     odd = lax.rem(refs.pop(0)[0], 2) == 1
     even_own, odd_own, rest_ref, even_ref, odd_ref = (refs.pop(0) for _ in range(5))
     x_ref, y_ref, turn_ref, land_ref = (refs.pop(0) for _ in range(4))
-    if chunk:
-        refs.pop(0)
-    out_ref, cells, work, moved, packed, trig, sems = refs
+    if final:
+        out_ref, cells, work, moved, trig, packed, sems = refs[-7:]
+    else:
+        even_out, odd_out, cells, work, moved, trig = refs
     rows = 4
     tiles = freqs // TILE
     half_turn = ND // 2
@@ -519,32 +563,56 @@
 
     every_class(tiles, only_pass)
 
-    @pl.loop(0, tiles * 4)
-    def _(i):
-        t = i // 4
-        r = lax.rem(i, 4)
-
-        def put(d, value):
-            packed[r, pl.ds(t * (TILE * ND) + d, TILE, stride=ND), :] = value
-
-        turn_rows(
-            [
-                (
-                    lambda d: work[t, r, d],
-                    lambda d: turn_ref[chunk * tiles + t, (r + 2) * half_turn + d],
-                    land_ref[r + 2],
-                    put,
-                )
-            ]
-        )
-
-    run_copies(
-        [
-            (packed.at[r], out_ref.at[pl.ds(chunk * span, span), pl.ds(r * LANES, LANES)])
-            for r in range(rows)
-        ],
-        sems,
-    )
+    @pl.loop(0, rows)
+    def _(r):
+        @pl.loop(0, tiles)
+        def _(t):
+            def put(d, value):
+                if final:
+                    packed[r, pl.ds(t * (TILE * ND) + d, TILE, stride=ND), :] = value
+                else:
+                    cells[t, r + 2, d] = value
+
+            turn_rows(
+                [
+                    (
+                        lambda d: work[t, r, d],
+                        lambda d: turn_ref[chunk * tiles + t, (r + 2) * half_turn + d],
+                        land_ref[r + 2],
+                        put,
+                    )
+                ]
+            )
+
+        if final:
+            output_row(packed, out_ref, chunk * span, span, r, sems).start()
+
+    if final:
+        for r in range(rows):
+            output_row(packed, out_ref, chunk * span, span, r, sems).wait()
+        return
+
+    def hand_out(up_out, down_out):
+        @pl.loop(0, ND)
+        def _(d):
+            for t, part in enumerate(parts):
+                for k in range(2):
+                    up_out[k * ND + d, part, :] = cells[t, 5 - k, d]
+                    down_out[k * ND + d, part, :] = cells[t, 2 + k, d]
+
+        @pl.loop(0, 22)
+        def _(i):
+            for t, part in enumerate(parts):
+                up_out[THIRD + i, part, :] = cells[t, 3, lax.rem(i + 26, ND)]
+                down_out[THIRD + i, part, :] = cells[t, 4, i + 8]
+
+        @pl.loop(0, 18)
+        def _(i):
+            for t, part in enumerate(parts):
+                up_out[FOURTH + i, part, :] = cells[t, 2, lax.rem(i + 28, ND)]
+                down_out[FOURTH + i, part, :] = cells[t, 5, i + 10]
+
+    by_parity(odd, lambda: hand_out(even_out, odd_out), lambda: hand_out(odd_out, even_out))
 
 
 def cost(flops, size):
@@ -578,6 +646,7 @@
     steps = list(zip(order[:-1], order[1:]))
     even_swaps = [swap for i, j in steps[0::2] for swap in ((i, j), (j, i))]
     odd_swaps = [swap for i, j in steps[1::2] for swap in ((i, j), (j, i))]
+    strip_swaps = [swap for i, j in steps[comps - 1 :: comps] for swap in ((i, j), (j, i))]
     block_index = lax.axis_index("space") * comps + lax.axis_index("comp")
     block_index = block_index.astype(jnp.int32).reshape(1)
     scalar = pl.BlockSpec(memory_space=pltpu.SMEM)
@@ -598,8 +667,10 @@
 
     def source(chunk):
         last = chunk == CHUNKS - 1
-        shapes = [tiles(TWO + (1 if chunk == 0 else 0))] * 2
-        operands = [spectrum, wind_field, coupling, growth, dissipation, sea_mask, depth_index]
+        wide = WIDE_FIRST[chunk]
+        shapes = [tiles(TWO)] * 2 if wide else [tiles(ONE), tiles(ONE), tiles(ND)]
+        out_specs = [far] * len(shapes)
+        operands = [spectrum, wind_field, coupling, growth, dissipation]
         scratch = [like(shape) for shape in shapes] + [
             pltpu.VMEM((rows, components, LANES), jnp.float32),
             like(wind_field),
@@ -608,19 +679,19 @@
             like(dissipation),
             pltpu.VMEM((components, points), jnp.bfloat16),
             pltpu.VMEM((rows, span, LANES), jnp.float32),
-            like(sea_mask),
-            like(depth_index),
-            pltpu.SemaphoreType.DMA((14,)),
+            pltpu.SemaphoreType.DMA((13,)),
+            pltpu.SemaphoreType.DMA((4,)),
         ]
         if last:
-            shapes.append(block(2 * nfreq + 2 * TILE, LANES))
-            more = [depths, group_speed, refraction]
+            shapes += [block(2 * nfreq + 5 * TILE, LANES), block(TILE, LANES)]
+            out_specs += [near, near]
+            more = [sea_mask, depth_index, depths, group_speed, refraction]
             operands += more
-            scratch += [like(shapes[2])] + [like(a) for a in more]
+            scratch += [like(a) for a in more]
         return pl.pallas_call(
-            functools.partial(source_kernel, chunk, freqs, last, comps),
+            functools.partial(source_kernel, chunk, freqs, wide, last, comps),
             in_specs=[scalar] + [far] * len(operands),
-            out_specs=[far] * len(shapes),
+            out_specs=out_specs,
             out_shape=shapes,
             scratch_shapes=scratch,
             compiler_params=params(57 if chunk else 63),
@@ -628,7 +699,7 @@
             name="source_terms",
         )(block_index, *operands)
 
-    def coast(even, odd, kit):
+    def coast(edge, kit):
         shapes = [
             block(rows + 5, nfreq, LANES),
             block(rows + 4, nfreq, LANES),
@@ -637,14 +708,14 @@
         ]
         return pl.pallas_call(
             functools.partial(coast_kernel, nfreq),
-            in_specs=[scalar] + [near] * 3,
+            in_specs=[scalar] + [near] * 2,
             out_specs=[near] * len(shapes),
             out_shape=shapes,
             scratch_shapes=[pltpu.VMEM((2 * (rows + 4), nfreq, LANES), jnp.float32)],
             compiler_params=params(24),
             cost_estimate=cost(ND * rows * nfreq * LANES, 4 * ND * rows * nfreq * LANES),
             name="coast_tables",
-        )(block_index, even, odd, kit)
+        )(block_index, edge, kit)
 
     def exchange(even, odd):
         odd = lax.ppermute(odd, BLOCKS, odd_swaps)
@@ -656,65 +727,70 @@
 
     trig = pltpu.SMEM((2, CLASSES), jnp.float32)
 
-    def two_steps(chunk, state, halo, tables):
-        operands = [block_index, *state, *halo, *tables]
-        shapes = [tiles(ONE), tiles(ONE), tiles(ND)]
-        return pl.pallas_call(
-            functools.partial(two_steps_kernel, chunk, freqs),
-            in_specs=[scalar] + [near] * (len(operands) - 1),
-            out_specs=[near] * len(shapes),
-            out_shape=shapes,
-            scratch_shapes=[
-                pltpu.VMEM((2, freqs // TILE, rows + 8, ND, TILE, LANES), jnp.float32),
-                work,
-                passed,
-                trig,
-            ],
-            compiler_params=params(24),
-            cost_estimate=cost(3 * 40 * span * points, 4 * 4 * span * points),
-            name="two_substeps",
-        )(*operands)
-
-    def last_step(chunk, state, halo, tables, out):
+    def advance(kernel, name, chunk, state, halo, tables, shapes, buffers, out):
         operands = [block_index, *state, *halo, *tables]
         specs = [scalar] + [near] * (len(operands) - 1)
+        scratch = [*buffers, work, passed, trig]
         aliases = {}
-        if out is not None:
-            aliases = {len(operands): 0}
-            operands.append(out)
-            specs.append(far)
+        final = not shapes
+        if final:
+            shapes = [block(*spectrum.shape)]
+            scratch += [
+                pltpu.VMEM((rows, span, LANES), jnp.float32),
+                pltpu.SemaphoreType.DMA((rows,)),
+            ]
+            if out is not None:
+                aliases = {len(operands): 0}
+                operands.append(out)
+                specs.append(far)
         return pl.pallas_call(
-            functools.partial(last_step_kernel, chunk, freqs),
+            functools.partial(kernel, chunk, freqs, final),
             in_specs=specs,
-            out_specs=far,
-            out_shape=block(*spectrum.shape),
-            scratch_shapes=[
-                pltpu.VMEM((freqs // TILE, rows + 4, ND, TILE, LANES), jnp.float32),
-                work,
-                passed,
-                pltpu.VMEM((rows, span, LANES), jnp.float32),
-                trig,
-                pltpu.SemaphoreType.DMA((rows,)),
-            ],
+            out_specs=[far if final else near] * len(shapes),
+            out_shape=shapes,
+            scratch_shapes=scratch,
             input_output_aliases=aliases,
             compiler_params=params(24),
-            cost_estimate=cost(40 * span * points, 4 * 4 * span * points),
-            name="last_substep",
+            cost_estimate=cost(2 * 40 * span * points, 4 * 4 * span * points),
+            name=name,
         )(*operands)
 
+    groups = freqs // TILE
+
+    def two_steps(chunk, state, halo, tables, shapes=(), out=None):
+        buffers = [pltpu.VMEM((2, groups, rows + 8, ND, TILE, LANES), jnp.float32)]
+        name = "two_substeps"
+        return advance(
+            two_steps_kernel, name, chunk, state, halo, tables, shapes, buffers, out
+        )
+
+    def one_step(chunk, state, halo, tables, shapes=(), out=None):
+        buffers = [pltpu.VMEM((groups, rows + 4, ND, TILE, LANES), jnp.float32)]
+        name = "one_substep"
+        return advance(
+            one_step_kernel, name, chunk, state, halo, tables, shapes, buffers, out
+        )
+
+    narrow = [tiles(ONE), tiles(ONE), tiles(ND)]
     states = []
     halos = []
     for chunk in range(CHUNKS):
-        even, odd, *kit = source(chunk)
-        states.append((even, odd))
+        even, odd, *more = source(chunk)
+        states.append((even, odd) if WIDE_FIRST[chunk] else (even, odd, more[0]))
         halos.append(exchange(even, odd))
-    tables = coast(*halos[0], *kit)
+    kit, edge = more[-2:]
+    tables = coast(lax.ppermute(edge, BLOCKS, strip_swaps), kit)
     for chunk in range(CHUNKS):
-        states[chunk] = two_steps(chunk, states[chunk], halos[chunk], tables)
-        halos[chunk] = exchange(*states[chunk][:2])
+        if WIDE_FIRST[chunk]:
+            made = two_steps(chunk, states[chunk], halos[chunk], tables, narrow)
+        else:
+            made = one_step(chunk, states[chunk], halos[chunk], tables, [tiles(TWO)] * 2)
+        states[chunk] = made
+        halos[chunk] = exchange(*made[:2])
     out = None
     for chunk in range(CHUNKS):
-        out = last_step(chunk, states[chunk], halos[chunk], tables, out)
+        step = one_step if WIDE_FIRST[chunk] else two_steps
+        (out,) = step(chunk, states[chunk], halos[chunk], tables, out=out)
     return out
 
 

time: 84.7 us -> 79.6 us (0.940)
  waiting for transfers between devices: 28.1 us -> 21.3 us
  Pallas kernels: 39.2 us -> 40.3 us
    ppermute x4, waiting for transfers between devices: 28.1 us -> 21.3 us  [exchange(): odd = lax.ppermute(odd, BLOCKS, odd_swaps)]
    pallas_call x6, Pallas kernels: 38.3 us -> 39.3 us  [the longest x4 29.6 us: advance(): pl.pallas_call(functools.partial(kernel, chunk, freqs, final), in_specs=s...]
  transfers between devices with their start and end apart: 8 -> 9, of which waited for: 2 -> 2; matrix products, arithmetic and copies ran while one was open for 0% -> 0% of each run, Pallas kernels for 36% -> 40%
where the time goes in v3:
time: 79.6 us; the launch traced here: 78.8 us
  Pallas kernels  40.3 us (51%)
  waiting for transfers between devices  21.3 us (27%)
  starting transfers between devices  16.1 us (20%)
  local copies, waits for them, and re-layouts  0.83 us (1%)
    pallas_call x4, Pallas kernels, advance(): pl.pallas_call(functools.partial(kernel, chunk, freqs, final), in_specs=s...  29.6 us
    ppermute x4, waiting for transfers between devices, exchange(): odd = lax.ppermute(odd, BLOCKS, odd_swaps)  21.3 us
    ppermute x4, starting transfers between devices, exchange(): odd = lax.ppermute(odd, BLOCKS, odd_swaps)  15.1 us
    pallas_call x2, Pallas kernels, source(): pl.pallas_call(functools.partial(source_kernel, chunk, freqs, wide, last,...  9.74 us
  transfers between devices with their start and end apart: 9, of which 2 were waited for; matrix products, arithmetic and copies ran while one was open for 0% of the time, Pallas kernels for 40%

profile of v3, /device:TPU:1, one launch (start us, length us, event | category | flops | bytes accessed | tf_op | source)
XLA Modules:
  0.0 78.8 jit_solution(17172951832843159558)
XLA Ops:
  0.0 4.4 %source_terms.3 = (f32[54,16,128]{2,1,0:T(8,128)}, f32[54,16,128]{2,1,0:T(8,128)}, f32[36,16,128]{2,1,0:T(8,128)}) custom-call(s32[1]{0:T(128)} %bitcast.refs_0_.block_ref, f32[1152,512]{1,0:T(8,128)} %refs_1_.3, f32[2,512]{1,0:T(2,128)} %refs_2_.3, bf16[1152,1152]{1,0:T(8,128)(2,1)} %refs_3_.3, f32[1,32]{1,0:T(1,128)} %bitcast.4, f32[1,32]{1,0:T(1,128)} %bitcast.6), custom_call_target="tpu_custom_call" | custom-call | flops 679477248 | bytes 2359296 | tf_op jit(solution)/shard_map/source_terms/pallas_call | solution.py:691
  4.4 0.1 collective-permute-start.5
  4.5 4.5 %collective-permute-start.6 = (f32[54,16,128]{2,1,0:T(8,128)}, f32[54,16,128]{2,1,0:T(8,128)S(1)}, u32[]{:S(2)}, u32[]{:S(2)}) collective-permute-start(f32[54,16,128]{2,1,0:T(8,128)} %get-tuple-element.33.refs_2_), channel_id=1, source_target_pairs={{2,4},{4,2},{6,8},{8,6},{10,12},{12,10},{14,16},{16,14},{18,20},{2... | collective-permute-start | bytes 1327112 | tf_op jit(solution)/shard_map/ppermute | solution.py:721
  9.0 0.0 copy-start.2
  9.0 0.0 copy-start.3
  9.0 0.0 copy-start.4
  9.0 5.4 %source_terms.2 = (f32[112,16,128]{2,1,0:T(8,128)}, f32[112,16,128]{2,1,0:T(8,128)}, f32[104,128]{1,0:T(8,128)}, f32[8,128]{1,0:T(8,128)}) custom-call(s32[1]{0:T(128)} %bitcast.refs_0_.block_ref, f32[1152,512]{1,0:T(8,128)} %refs_1_.3, f32[2,512]{1,0:T(2,128)} %refs_2_.3, bf16[1152,1152]{1,0:T(8,128)(2,1)} %refs_3_.3, f32[1,32]{1,0:T(1,128)} %bitcast.5, ...), custom_call_target="tpu_custom_call" | custom-call | flops 679477248 | bytes 2359296 | tf_op jit(solution)/shard_map/source_terms/pallas_call | solution.py:691
  14.4 0.1 collective-permute-start
  14.5 3.5 %collective-permute-start.1 = (f32[112,16,128]{2,1,0:T(8,128)}, f32[112,16,128]{2,1,0:T(8,128)S(1)}, u32[]{:S(2)}, u32[]{:S(2)}) collective-permute-start(f32[112,16,128]{2,1,0:T(8,128)} %get-tuple-element.22.refs_2_), channel_id=1, source_target_pairs={{2,4},{4,2},{6,8},{8,6},{10,12},{12,10},{14,16},{16,14},{18,20},{2... | collective-permute-start | bytes 2752520 | tf_op jit(solution)/shard_map/ppermute | solution.py:721
  18.0 0.7 collective-permute-start.2
  18.7 0.0 collective-permute-done.2.far_ref
  18.7 0.0 copy-start.5
  18.7 0.8 %copy-done.5 = f32[104,128]{1,0:T(8,128)S(1)} copy-done((f32[104,128]{1,0:T(8,128)S(1)}, f32[104,128]{1,0:T(8,128)}, u32[]{:S(2)}) %copy-start.5) | copy-done | bytes 53272
  19.5 1.0 %coast_tables.1 = (f32[9,32,128]{2,1,0:T(8,128)S(1)}, f32[8,32,128]{2,1,0:T(8,128)S(1)}, f32[4,144,8,128]{3,2,1,0:T(8,128)S(1)}, f32[8,8,128]{2,1,0:T(8,128)S(1)}) custom-call(s32[1]{0:T(128)} %bitcast.refs_0_.block_ref, f32[8,128]{1,0:T(8,128)S(1)} %collective-permute-done.2.far_ref, f32[104,128]{1,0:T(8,128)S(1)} %copy-done.5), custom_call_target="tpu_custom_call" | custom-call | flops 589824 | bytes 2359296 | tf_op jit(solution)/shard_map/coast_tables/pallas_call | solution.py:709
  20.5 0.0 collective-permute-done.5.refs_4_
  20.5 0.0 collective-permute-done.6.refs_5_
  20.5 0.0 copy-done.2
  20.5 0.0 copy-done.3
  20.5 0.0 copy-done.4
  20.5 0.0 copy-start
  20.6 0.0 copy-start.1
  20.6 4.1 %one_substep.2 = (f32[112,16,128]{2,1,0:T(8,128)S(1)}, f32[112,16,128]{2,1,0:T(8,128)S(1)}) custom-call(s32[1]{0:T(128)} %bitcast.refs_0_.block_ref, f32[54,16,128]{2,1,0:T(8,128)S(1)} %copy-done.2, f32[54,16,128]{2,1,0:T(8,128)S(1)} %copy-done.3, f32[36,16,128]{2,1,0:T(8,128)S(1)} %copy-done.4, f32[54,16,128]{2,1,0:T(8,128)S(1)} %collective-permute-done.5.refs_4_, ...), custom_call_target="tpu_custom_call" | custom-call | flops 23592960 | bytes 4718592 | tf_op jit(solution)/shard_map/one_substep/pallas_call | solution.py:746
  24.7 0.1 collective-permute-start.7
  24.7 3.5 %collective-permute-start.8 = (f32[112,16,128]{2,1,0:T(8,128)S(1)}, f32[112,16,128]{2,1,0:T(8,128)S(1)}, u32[]{:S(2)}, u32[]{:S(2)}) collective-permute-start(f32[112,16,128]{2,1,0:T(8,128)S(1)} %get-tuple-element.36.refs_2_), channel_id=1, source_target_pairs={{2,4},{4,2},{6,8},{8,6},{10,12},{12,10},{14,16},{16,14},{18,20},{2... | collective-permute-start | bytes 2752520 | tf_op jit(solution)/shard_map/ppermute | solution.py:721
  28.2 0.0 collective-permute-done.refs_3_
  28.3 11.4 %collective-permute-done.1.refs_4_ = f32[112,16,128]{2,1,0:T(8,128)S(1)} collective-permute-done((f32[112,16,128]{2,1,0:T(8,128)}, f32[112,16,128]{2,1,0:T(8,128)S(1)}, u32[]{:S(2)}, u32[]{:S(2)}) %collective-permute-start.1) | collective-permute-done | bytes 917536 | tf_op jit(solution)/shard_map/ppermute | solution.py:721
  39.6 0.0 copy-done
  39.6 0.0 copy-done.1
  39.6 9.9 %two_substeps.2 = (f32[54,16,128]{2,1,0:T(8,128)S(1)}, f32[54,16,128]{2,1,0:T(8,128)S(1)}, f32[36,16,128]{2,1,0:T(8,128)S(1)}) custom-call(s32[1]{0:T(128)} %bitcast.refs_0_.block_ref, f32[112,16,128]{2,1,0:T(8,128)S(1)} %copy-done, f32[112,16,128]{2,1,0:T(8,128)S(1)} %copy-done.1, f32[112,16,128]{2,1,0:T(8,128)S(1)} %collective-permute-done.refs_3_, ...), custom_call_target="tpu_custom_call" | custom-call | flops 23592960 | bytes 4718592 | tf_op jit(solution)/shard_map/two_substeps/pallas_call | solution.py:746
  49.6 0.1 collective-permute-start.3
  49.7 3.6 %collective-permute-start.4 = (f32[54,16,128]{2,1,0:T(8,128)S(1)}, f32[54,16,128]{2,1,0:T(8,128)S(1)}, u32[]{:S(2)}, u32[]{:S(2)}) collective-permute-start(f32[54,16,128]{2,1,0:T(8,128)S(1)} %get-tuple-element.30.refs_2_), channel_id=1, source_target_pairs={{2,4},{4,2},{6,8},{8,6},{10,12},{12,10},{14,16},{16,14},{18,20},{2... | collective-permute-start | bytes 1327112 | tf_op jit(solution)/shard_map/ppermute | solution.py:721
  53.3 0.0 collective-permute-done.7.refs_3_
  53.3 9.9 %collective-permute-done.8.refs_4_ = f32[112,16,128]{2,1,0:T(8,128)S(1)} collective-permute-done((f32[112,16,128]{2,1,0:T(8,128)S(1)}, f32[112,16,128]{2,1,0:T(8,128)S(1)}, u32[]{:S(2)}, u32[]{:S(2)}) %collective-permute-start.8) | collective-permute-done | bytes 917536 | tf_op jit(solution)/shard_map/ppermute | solution.py:721
  63.2 11.4 %two_substeps.3.refs_10_ = f32[1152,512]{1,0:T(8,128)} custom-call(s32[1]{0:T(128)} %bitcast.refs_0_.block_ref, f32[112,16,128]{2,1,0:T(8,128)S(1)} %get-tuple-element.35.refs_1_, f32[112,16,128]{2,1,0:T(8,128)S(1)} %get-tuple-element.36.refs_2_, f32[112,16,128]{2,1,0:T(8,128)S(1)} %collective-permute-done.7.refs_3_, ...), custom_call_target="tpu_custom_call" | custom-call | flops 23592960 | bytes 4718592 | tf_op jit(solution)/shard_map/two_substeps/pallas_call | solution.py:746
  74.6 0.0 collective-permute-done.3.refs_4_
  74.6 0.0 collective-permute-done.4.refs_5_
  74.6 4.2 %one_substep.3 = f32[1152,512]{1,0:T(8,128)} custom-call(s32[1]{0:T(128)} %bitcast.refs_0_.block_ref, f32[54,16,128]{2,1,0:T(8,128)S(1)} %get-tuple-element.29.refs_1_, f32[54,16,128]{2,1,0:T(8,128)S(1)} %get-tuple-element.30.refs_2_, f32[36,16,128]{2,1,0:T(8,128)S(1)} %get-tuple-element.31.refs_3_, ...), custom_call_target="tpu_custom_call", output_to_operand_aliasing={{}: (10, {})} | custom-call | flops 23592960 | bytes 4718592 | tf_op jit(solution)/shard_map/one_substep/pallas_call | solution.py:746
Async XLA Ops:
  4.4 16.1 %collective-permute-start.5 = (f32[54,16,128]{2,1,0:T(8,128)}, f32[54,16,128]{2,1,0:T(8,128)S(1)}, u32[]{:S(2)}, u32[]{:S(2)}) collective-permute-start(f32[54,16,128]{2,1,0:T(8,128)} %get-tuple-element.32.refs_1_), channel_id=1, source_target_pairs={{0,2},{2,0},{4,6},{6,4},{8,10},{10,8},{12,14},{14,12},{16,18},{18,... | collective-permute-start | bytes 1327112 | tf_op jit(solution)/shard_map/ppermute | solution.py:722
  4.5 16.0 %collective-permute-start.6 = (f32[54,16,128]{2,1,0:T(8,128)}, f32[54,16,128]{2,1,0:T(8,128)S(1)}, u32[]{:S(2)}, u32[]{:S(2)}) collective-permute-start(f32[54,16,128]{2,1,0:T(8,128)} %get-tuple-element.33.refs_2_), channel_id=1, source_target_pairs={{2,4},{4,2},{6,8},{8,6},{10,12},{12,10},{14,16},{16,14},{18,20},{2... | collective-permute-start | bytes 1327112 | tf_op jit(solution)/shard_map/ppermute | solution.py:721
  9.0 11.5 %copy-start.2 = (f32[54,16,128]{2,1,0:T(8,128)S(1)}, f32[54,16,128]{2,1,0:T(8,128)}, u32[]{:S(2)}) copy-start(f32[54,16,128]{2,1,0:T(8,128)} %get-tuple-element.32.refs_1_) | copy-start | bytes 1327108
  9.0 11.5 %copy-start.3 = (f32[54,16,128]{2,1,0:T(8,128)S(1)}, f32[54,16,128]{2,1,0:T(8,128)}, u32[]{:S(2)}) copy-start(f32[54,16,128]{2,1,0:T(8,128)} %get-tuple-element.33.refs_2_) | copy-start | bytes 1327108
  9.0 11.5 %copy-start.4 = (f32[36,16,128]{2,1,0:T(8,128)S(1)}, f32[36,16,128]{2,1,0:T(8,128)}, u32[]{:S(2)}) copy-start(f32[36,16,128]{2,1,0:T(8,128)} %get-tuple-element.34.refs_3_) | copy-start | bytes 884740
  14.4 13.8 %collective-permute-start = (f32[112,16,128]{2,1,0:T(8,128)}, f32[112,16,128]{2,1,0:T(8,128)S(1)}, u32[]{:S(2)}, u32[]{:S(2)}) collective-permute-start(f32[112,16,128]{2,1,0:T(8,128)} %get-tuple-element.21.refs_1_), channel_id=1, source_target_pairs={{0,2},{2,0},{4,6},{6,4},{8,10},{10,8},{12,14},{14,12},{16,18},{18,... | collective-permute-start | bytes 2752520 | tf_op jit(solution)/shard_map/ppermute | solution.py:722
  14.5 25.1 %collective-permute-start.1 = (f32[112,16,128]{2,1,0:T(8,128)}, f32[112,16,128]{2,1,0:T(8,128)S(1)}, u32[]{:S(2)}, u32[]{:S(2)}) collective-permute-start(f32[112,16,128]{2,1,0:T(8,128)} %get-tuple-element.22.refs_2_), channel_id=1, source_target_pairs={{2,4},{4,2},{6,8},{8,6},{10,12},{12,10},{14,16},{16,14},{18,20},{2... | collective-permute-start | bytes 2752520 | tf_op jit(solution)/shard_map/ppermute | solution.py:721
  18.0 0.7 collective-permute-start.2
  18.7 0.8 %copy-start.5 = (f32[104,128]{1,0:T(8,128)S(1)}, f32[104,128]{1,0:T(8,128)}, u32[]{:S(2)}) copy-start(f32[104,128]{1,0:T(8,128)} %get-tuple-element.24.kit_ref) | copy-start | bytes 159748
  20.5 19.1 %copy-start = (f32[112,16,128]{2,1,0:T(8,128)S(1)}, f32[112,16,128]{2,1,0:T(8,128)}, u32[]{:S(2)}) copy-start(f32[112,16,128]{2,1,0:T(8,128)} %get-tuple-element.21.refs_1_) | copy-start | bytes 2752516
  20.6 19.1 %copy-start.1 = (f32[112,16,128]{2,1,0:T(8,128)S(1)}, f32[112,16,128]{2,1,0:T(8,128)}, u32[]{:S(2)}) copy-start(f32[112,16,128]{2,1,0:T(8,128)} %get-tuple-element.22.refs_2_) | copy-start | bytes 2752516
  24.7 28.6 %collective-permute-start.7 = (f32[112,16,128]{2,1,0:T(8,128)S(1)}, f32[112,16,128]{2,1,0:T(8,128)S(1)}, u32[]{:S(2)}, u32[]{:S(2)}) collective-permute-start(f32[112,16,128]{2,1,0:T(8,128)S(1)} %get-tuple-element.35.refs_1_), channel_id=1, source_target_pairs={{0,2},{2,0},{4,6},{6,4},{8,10},{10,8},{12,14},{14,12},{16,18},{18,... | collective-permute-start | bytes 2752520 | tf_op jit(solution)/shard_map/ppermute | solution.py:722
  24.7 38.5 %collective-permute-start.8 = (f32[112,16,128]{2,1,0:T(8,128)S(1)}, f32[112,16,128]{2,1,0:T(8,128)S(1)}, u32[]{:S(2)}, u32[]{:S(2)}) collective-permute-start(f32[112,16,128]{2,1,0:T(8,128)S(1)} %get-tuple-element.36.refs_2_), channel_id=1, source_target_pairs={{2,4},{4,2},{6,8},{8,6},{10,12},{12,10},{14,16},{16,14},{18,20},{2... | collective-permute-start | bytes 2752520 | tf_op jit(solution)/shard_map/ppermute | solution.py:721
  49.6 25.0 %collective-permute-start.3 = (f32[54,16,128]{2,1,0:T(8,128)S(1)}, f32[54,16,128]{2,1,0:T(8,128)S(1)}, u32[]{:S(2)}, u32[]{:S(2)}) collective-permute-start(f32[54,16,128]{2,1,0:T(8,128)S(1)} %get-tuple-element.29.refs_1_), channel_id=1, source_target_pairs={{0,2},{2,0},{4,6},{6,4},{8,10},{10,8},{12,14},{14,12},{16,18},{18,... | collective-permute-start | bytes 1327112 | tf_op jit(solution)/shard_map/ppermute | solution.py:722
  49.7 25.0 %collective-permute-start.4 = (f32[54,16,128]{2,1,0:T(8,128)S(1)}, f32[54,16,128]{2,1,0:T(8,128)S(1)}, u32[]{:S(2)}, u32[]{:S(2)}) collective-permute-start(f32[54,16,128]{2,1,0:T(8,128)S(1)} %get-tuple-element.30.refs_2_), channel_id=1, source_target_pairs={{2,4},{4,2},{6,8},{8,6},{10,12},{12,10},{14,16},{16,14},{18,20},{2... | collective-permute-start | bytes 1327112 | tf_op jit(solution)/shard_map/ppermute | solution.py:721

commit v4 on v3

--- a/solution.py
+++ b/solution.py
@@ -95,17 +95,19 @@
     refs = list(refs)
     rows = 4
     block = refs.pop(0)[0]
-    spectrum, wind, coupling, growth_in, dissipation_in = (refs.pop(0) for _ in range(5))
+    spectrum, wind, coupling, growth_in, dissipation_in, mask_in, index_in = (
+        refs.pop(0) for _ in range(7)
+    )
     if last:
-        coast_in = [refs.pop(0) for _ in range(5)]
+        tables_in = [refs.pop(0) for _ in range(3)]
     even_out, odd_out = refs.pop(0), refs.pop(0)
     if not wide:
         rest_out = refs.pop(0)
     if last:
-        kit, edge = refs.pop(0), refs.pop(0)
+        kit = refs.pop(0)
     outs = [refs.pop(0) for _ in range(2 if wide else 3)]
     spec, wind_ref, operator, growth_ref, dissipation_ref, rounded, mixed = refs[:7]
-    sems, out_sems = refs[7:9]
+    mask_ref, index_ref, sems, out_sems = refs[7:11]
     span = freqs * ND
     pairs = [(spectrum.at[:, pl.ds(r * LANES, LANES)], spec.at[r]) for r in range(rows)]
     pairs += [
@@ -113,10 +115,12 @@
         (wind, wind_ref),
         (growth_in, growth_ref),
         (dissipation_in, dissipation_ref),
+        (mask_in, mask_ref),
+        (index_in, index_ref),
     ]
     if last:
-        mask_ref, index_ref, depths_ref, speed_ref, refraction_ref = refs[9:]
-        pairs += list(zip(coast_in, refs[9:]))
+        depths_ref, speed_ref, refraction_ref = refs[11:]
+        pairs += list(zip(tables_in, refs[11:]))
     copies = fetch(pairs, sems)
     for r in range(rows):
         copies[r].wait()
@@ -145,6 +149,15 @@
         )
         return pltpu.make_async_copy(outs[which].at[part], even_out.at[part], out_sems.at[number])
 
+    first = lax.rem(block, comps) * rows
+    mask = mask_ref[...].astype(jnp.float32)
+    index = index_ref[...].astype(jnp.float32)
+    if not wide:
+        near_side = first + jnp.where(odd, rows - 3, 0)
+        edge = [pick_row(strip, near_side + k) for strip in (mask, index) for k in range(3)]
+        edge = jnp.concatenate(edge + [jnp.zeros((freqs - 6, LANES), jnp.float32)], axis=0)
+        outs[0][ONE] = edge
+        outs[1][ONE] = edge
     for r in (3, 2, 1, 0):
         average = jnp.sum(spec[r], axis=0, keepdims=True) * (1.0 / components)
         limited = average / (average + 1.0)
@@ -169,17 +182,14 @@
         if r == 2 and wide:
             leaving = [leave(0, 0, 0, THIRD), leave(1, 1, THIRD, TWO - THIRD)]
         elif r == 2:
-            leaving = [leave(0, 0, 0, ONE)]
+            leaving = [leave(0, 0, 0, ONE + 1)]
     if wide:
         leaving += [leave(2, 1, 0, THIRD), leave(3, 0, THIRD, TWO - THIRD)]
     else:
         rest_copy = pltpu.make_async_copy(outs[2], rest_out, out_sems.at[2])
         rest_copy.start()
-        leaving += [leave(1, 1, 0, ONE), rest_copy]
+        leaving += [leave(1, 1, 0, ONE + 1), rest_copy]
     if last:
-        first = lax.rem(block, comps) * rows
-        mask = mask_ref[...].astype(jnp.float32)
-        index = index_ref[...].astype(jnp.float32)
         count, levels = speed_ref.shape
         kit[...] = jnp.zeros_like(kit)
         kit[:count, :levels] = speed_ref[...]
@@ -188,11 +198,6 @@
         for k in range(rows + 6):
             kit[2 * count + TILE + k, :] = pick_row(mask, first + k - 3)[0]
             kit[2 * count + 3 * TILE + k, :] = pick_row(index, first + k - 3)[0]
-        near_side = first + jnp.where(odd, rows - 3, 0)
-        edge[...] = jnp.zeros_like(edge)
-        for k in range(3):
-            edge[k, :] = pick_row(mask, near_side + k)[0]
-            edge[3 + k, :] = pick_row(index, near_side + k)[0]
     for copy in leaving:
         copy.wait()
 
@@ -207,18 +212,20 @@
 
 
 def coast_kernel(
-    count, block_ref, far_ref, kit_ref, face_x, face_y, turn_ref, land_ref, slope_by
+    count, comps, block_ref, far_ref, kit_ref, face_x, face_y, turn_ref, land_ref, slope_by
 ):
     rows = 4
     tables = kit_ref[: 2 * count + TILE, :]
-    odd = (lax.rem(block_ref[0], 2) == 1).astype(jnp.float32)
+    place = lax.rem(block_ref[0], comps)
+    below = (place == 0).astype(jnp.float32)
+    above = (place == comps - 1).astype(jnp.float32)
 
     def with_far(start, part):
         found = [kit_ref[start + k : start + k + 1, :] for k in range(rows + 6)]
         for k in range(3):
-            far = far_ref[part + k : part + k + 1, :]
-            found[k] += far * (1.0 - odd)
-            found[rows + 3 + k] += far * odd
+            far = far_ref[ONE, part + k : part + k + 1, :]
+            found[k] += far * below
+            found[rows + 3 + k] += far * above
         return found
 
     masks = with_far(2 * count + TILE, 0)
@@ -393,7 +400,8 @@
 
 
 def two_steps_kernel(chunk, freqs, final, *refs):
-    block_ref, even_own, odd_own, even_ref, odd_ref, x_ref, y_ref, turn_ref, land_ref = refs[:9]
+    block_ref, even_own, odd_own, *halo = refs[: 5 if final else 6]
+    x_ref, y_ref, turn_ref, land_ref = refs[3 + len(halo) : 7 + len(halo)]
     if final:
         out_ref, cells, work, moved, trig, packed, sems = refs[-7:]
     else:
@@ -405,7 +413,7 @@
     parts = [slice(t * TILE, (t + 1) * TILE) for t in range(tiles)]
 
     def gather(up_ref, down_ref, low_ref, high_ref):
-        @pl.loop(0, ND)
+        @pl.loop(0, ND, unroll=4)
         def _(d):
             for t, part in enumerate(parts):
                 for k in range(2):
@@ -414,23 +422,24 @@
                     cells[0, t, 7 - k, d] = up_ref[k * ND + d, part, :]
                     cells[0, t, 8 + k, d] = high_ref[k * ND + d, part, :]
 
-        @pl.loop(0, 22)
+        @pl.loop(0, 22, unroll=11)
         def _(i):
             for t, part in enumerate(parts):
                 cells[0, t, 1, lax.rem(i + 26, ND)] = low_ref[THIRD + i, part, :]
                 cells[0, t, 10, i + 8] = high_ref[THIRD + i, part, :]
 
-        @pl.loop(0, 18)
+        @pl.loop(0, 18, unroll=9)
         def _(i):
             for t, part in enumerate(parts):
                 cells[0, t, 0, lax.rem(i + 28, ND)] = low_ref[FOURTH + i, part, :]
                 cells[0, t, 11, i + 10] = high_ref[FOURTH + i, part, :]
 
-    by_parity(
-        odd,
-        lambda: gather(even_own, odd_own, odd_ref, even_ref),
-        lambda: gather(odd_own, even_own, even_ref, odd_ref),
-    )
+    even_ref, *odds = halo
+    for place in range(4):
+        odd_ref = odds[0] if place in (1, 2) else odds[-1]
+        low, high = (even_ref, odd_ref) if place % 2 else (odd_ref, even_ref)
+        own = (odd_own, even_own) if place % 2 else (even_own, odd_own)
+        pl.when(lax.rem(block_ref[0], 4) == place)(functools.partial(gather, *own, low, high))
 
     @pl.loop(0, 3)
     def _(stage):
@@ -476,7 +485,7 @@
 
         @pl.loop(0, rows)
         def _(r):
-            @pl.loop(0, ND)
+            @pl.loop(0, ND, unroll=6)
             def _(d):
                 for t in range(tiles):
                     place = pl.ds(t * (TILE * ND) + d, TILE, stride=ND)
@@ -489,13 +498,13 @@
         return
 
     def hand_out(up_out, down_out):
-        @pl.loop(0, ND)
+        @pl.loop(0, ND, unroll=4)
         def _(d):
             for t, part in enumerate(parts):
                 up_out[d, part, :] = cells[0, t, 7, d]
                 down_out[d, part, :] = cells[0, t, 4, d]
 
-        @pl.loop(0, half_turn)
+        @pl.loop(0, half_turn, unroll=6)
         def _(i):
             upward = lax.rem(i + 28, ND)
             for t, part in enumerate(parts):
@@ -524,7 +533,7 @@
     parts = [slice(t * TILE, (t + 1) * TILE) for t in range(tiles)]
 
     def gather(up_ref, down_ref, low_ref, high_ref):
-        @pl.loop(0, ND)
+        @pl.loop(0, ND, unroll=4)
         def _(d):
             for t, part in enumerate(parts):
                 cells[t, 1, d] = low_ref[d, part, :]
@@ -532,7 +541,7 @@
                 cells[t, 5, d] = up_ref[d, part, :]
                 cells[t, 6, d] = high_ref[d, part, :]
 
-        @pl.loop(0, half_turn)
+        @pl.loop(0, half_turn, unroll=6)
         def _(i):
             upward = lax.rem(i + 28, ND)
             for t, part in enumerate(parts):
@@ -593,20 +602,20 @@
         return
 
     def hand_out(up_out, down_out):
-        @pl.loop(0, ND)
+        @pl.loop(0, ND, unroll=4)
         def _(d):
             for t, part in enumerate(parts):
                 for k in range(2):
                     up_out[k * ND + d, part, :] = cells[t, 5 - k, d]
                     down_out[k * ND + d, part, :] = cells[t, 2 + k, d]
 
-        @pl.loop(0, 22)
+        @pl.loop(0, 22, unroll=11)
         def _(i):
             for t, part in enumerate(parts):
                 up_out[THIRD + i, part, :] = cells[t, 3, lax.rem(i + 26, ND)]
                 down_out[THIRD + i, part, :] = cells[t, 4, i + 8]
 
-        @pl.loop(0, 18)
+        @pl.loop(0, 18, unroll=9)
         def _(i):
             for t, part in enumerate(parts):
                 up_out[FOURTH + i, part, :] = cells[t, 2, lax.rem(i + 28, ND)]
@@ -646,7 +655,6 @@
     steps = list(zip(order[:-1], order[1:]))
     even_swaps = [swap for i, j in steps[0::2] for swap in ((i, j), (j, i))]
     odd_swaps = [swap for i, j in steps[1::2] for swap in ((i, j), (j, i))]
-    strip_swaps = [swap for i, j in steps[comps - 1 :: comps] for swap in ((i, j), (j, i))]
     block_index = lax.axis_index("space") * comps + lax.axis_index("comp")
     block_index = block_index.astype(jnp.int32).reshape(1)
     scalar = pl.BlockSpec(memory_space=pltpu.SMEM)
@@ -668,9 +676,9 @@
     def source(chunk):
         last = chunk == CHUNKS - 1
         wide = WIDE_FIRST[chunk]
-        shapes = [tiles(TWO)] * 2 if wide else [tiles(ONE), tiles(ONE), tiles(ND)]
+        shapes = [tiles(TWO)] * 2 if wide else [tiles(ONE + 1), tiles(ONE + 1), tiles(ND)]
         out_specs = [far] * len(shapes)
-        operands = [spectrum, wind_field, coupling, growth, dissipation]
+        operands = [spectrum, wind_field, coupling, growth, dissipation, sea_mask, depth_index]
         scratch = [like(shape) for shape in shapes] + [
             pltpu.VMEM((rows, components, LANES), jnp.float32),
             like(wind_field),
@@ -679,13 +687,15 @@
             like(dissipation),
             pltpu.VMEM((components, points), jnp.bfloat16),
             pltpu.VMEM((rows, span, LANES), jnp.float32),
+            like(sea_mask),
+            like(depth_index),
             pltpu.SemaphoreType.DMA((13,)),
             pltpu.SemaphoreType.DMA((4,)),
         ]
         if last:
-            shapes += [block(2 * nfreq + 5 * TILE, LANES), block(TILE, LANES)]
-            out_specs += [near, near]
-            more = [sea_mask, depth_index, depths, group_speed, refraction]
+            shapes += [block(2 * nfreq + 5 * TILE, LANES)]
+            out_specs += [near]
+            more = [depths, group_speed, refraction]
             operands += more
             scratch += [like(a) for a in more]
         return pl.pallas_call(
@@ -707,7 +717,7 @@
             block(rows + 4, TILE, LANES),
         ]
         return pl.pallas_call(
-            functools.partial(coast_kernel, nfreq),
+            functools.partial(coast_kernel, nfreq, comps),
             in_specs=[scalar] + [near] * 2,
             out_specs=[near] * len(shapes),
             out_shape=shapes,
@@ -720,6 +730,9 @@
     def exchange(even, odd):
         odd = lax.ppermute(odd, BLOCKS, odd_swaps)
         return lax.ppermute(even, BLOCKS, even_swaps), odd
+
+    first_swaps = [swap for i, j in steps[1::4] for swap in ((i, j), (j, i))]
+    later_swaps = [swap for i, j in steps[3::4] for swap in ((i, j), (j, i))]
 
     work = pltpu.VMEM((freqs // TILE, rows, ND + 1, TILE, LANES), jnp.float32)
 
@@ -774,12 +787,15 @@
     narrow = [tiles(ONE), tiles(ONE), tiles(ND)]
     states = []
     halos = []
-    for chunk in range(CHUNKS):
-        even, odd, *more = source(chunk)
-        states.append((even, odd) if WIDE_FIRST[chunk] else (even, odd, more[0]))
-        halos.append(exchange(even, odd))
-    kit, edge = more[-2:]
-    tables = coast(lax.ppermute(edge, BLOCKS, strip_swaps), kit)
+    even, odd, rest = source(0)
+    states.append((even, odd, rest))
+    halos.append(exchange(even, odd))
+    even, odd, kit = source(1)
+    states.append((even, odd))
+    tables = coast(halos[0][1], kit)
+    halo = [lax.ppermute(even, BLOCKS, even_swaps), lax.ppermute(odd, BLOCKS, first_swaps)]
+    odd, halos[0] = lax.optimization_barrier((odd, halos[0]))
+    halos.append((*halo, lax.ppermute(odd, BLOCKS, later_swaps)))
     for chunk in range(CHUNKS):
         if WIDE_FIRST[chunk]:
             made = two_steps(chunk, states[chunk], halos[chunk], tables, narrow)

time: 79.6 us -> 78 us (0.980)
  Pallas kernels: 40.3 us -> 37.6 us
  waiting for transfers between devices: 21.3 us -> 22.2 us
    ppermute x1 -> x3, waiting for transfers between devices: 0.01 us -> 19.8 us  [the longest x1 19.8 us: per_device(): lax.ppermute(odd, BLOCKS, first_swaps)]
    ppermute x4 -> x3, waiting for transfers between devices: 21.3 us -> 2.43 us  [exchange(): odd = lax.ppermute(odd, BLOCKS, odd_swaps)]
    ppermute x1 -> x3, starting transfers between devices: 0.66 us -> 4.33 us  [the longest x1 3.55 us: per_device(): lax.ppermute(odd, BLOCKS, first_swaps)]
    ppermute x4 -> x3, starting transfers between devices: 15.1 us -> 11.8 us  [exchange(): odd = lax.ppermute(odd, BLOCKS, odd_swaps)]
    pallas_call x4, Pallas kernels: 29.6 us -> 26.9 us  [advance(): pl.pallas_call(functools.partial(kernel, chunk, freqs, final), in_specs=s...]
  transfers between devices with their start and end apart: 9 -> 9, of which waited for: 2 -> 3; matrix products, arithmetic and copies ran while one was open for 0% -> 0% of each run, Pallas kernels for 40% -> 38%
where the time goes in v4:
time: 78 us; the launch traced here: 77.3 us
  Pallas kernels  37.6 us (48%)
  waiting for transfers between devices  22.2 us (28%)
  starting transfers between devices  16.4 us (21%)
  local copies, waits for them, and re-layouts  0.83 us (1%)
    pallas_call x4, Pallas kernels, advance(): pl.pallas_call(functools.partial(kernel, chunk, freqs, final), in_specs=s...  26.9 us
    ppermute x1, waiting for transfers between devices, per_device(): lax.ppermute(odd, BLOCKS, first_swaps)  19.8 us
    ppermute x3, starting transfers between devices, exchange(): odd = lax.ppermute(odd, BLOCKS, odd_swaps)  11.8 us
    pallas_call x2, Pallas kernels, source(): pl.pallas_call(functools.partial(source_kernel, chunk, freqs, wide, last,...  9.73 us
    ppermute x1, starting transfers between devices, per_device(): lax.ppermute(odd, BLOCKS, first_swaps)  3.55 us
    ppermute x3, waiting for transfers between devices, exchange(): odd = lax.ppermute(odd, BLOCKS, odd_swaps)  2.43 us
  transfers between devices with their start and end apart: 9, of which 3 were waited for; matrix products, arithmetic and copies ran while one was open for 0% of the time, Pallas kernels for 38%

profile of v4, /device:TPU:1, one launch (start us, length us, event | category | flops | bytes accessed | tf_op | source)
XLA Modules:
  0.0 77.3 jit_solution(9964553149678193685)
XLA Ops:
  0.0 4.4 %source_terms.3 = (f32[55,16,128]{2,1,0:T(8,128)}, f32[55,16,128]{2,1,0:T(8,128)}, f32[36,16,128]{2,1,0:T(8,128)}) custom-call(s32[1]{0:T(128)} %bitcast.refs_0_.block_ref, f32[1152,512]{1,0:T(8,128)} %refs_1_.3, f32[2,512]{1,0:T(2,128)} %refs_2_.3, bf16[1152,1152]{1,0:T(8,128)(2,1)} %refs_3_.3, f32[1,32]{1,0:T(1,128)} %bitcast.4, f32[1,32]{1,0:T(1,128)} %bitcast.6, ...), custom_call_target="tpu_custom_call" | custom-call | flops 679477248 | bytes 2359296 | tf_op jit(solution)/shard_map/source_terms/pallas_call | solution.py:701
  4.4 0.1 collective-permute-start.2
  4.5 4.5 %collective-permute-start.3 = (f32[55,16,128]{2,1,0:T(8,128)}, f32[55,16,128]{2,1,0:T(8,128)S(1)}, u32[]{:S(2)}, u32[]{:S(2)}) collective-permute-start(f32[55,16,128]{2,1,0:T(8,128)} %get-tuple-element.26.refs_2_), channel_id=1, source_target_pairs={{2,4},{4,2},{6,8},{8,6},{10,12},{12,10},{14,16},{16,14},{18,20},{2... | collective-permute-start | bytes 1351688 | tf_op jit(solution)/shard_map/ppermute | solution.py:731
  9.0 0.0 copy-start.2
  9.0 0.0 copy-start.3
  9.0 0.0 copy-start.4
  9.0 5.3 %source_terms.2 = (f32[112,16,128]{2,1,0:T(8,128)}, f32[112,16,128]{2,1,0:T(8,128)}, f32[104,128]{1,0:T(8,128)}) custom-call(s32[1]{0:T(128)} %bitcast.refs_0_.block_ref, f32[1152,512]{1,0:T(8,128)} %refs_1_.3, f32[2,512]{1,0:T(2,128)} %refs_2_.3, bf16[1152,1152]{1,0:T(8,128)(2,1)} %refs_3_.3, f32[1,32]{1,0:T(1,128)} %bitcast.5, f32[1,32]{1,0:T(1,128)} %bitcast.7, ...), custom_call_target="tpu_custom_call" | custom-call | flops 679477248 | bytes 2359296 | tf_op jit(solution)/shard_map/source_terms/pallas_call | solution.py:701
  14.4 0.1 collective-permute-start
  14.5 3.5 %collective-permute-start.1 = (f32[112,16,128]{2,1,0:T(8,128)}, f32[112,16,128]{2,1,0:T(8,128)S(1)}, u32[]{:S(2)}, u32[]{:S(2)}) collective-permute-start(f32[112,16,128]{2,1,0:T(8,128)} %get-tuple-element.27.refs_2_), channel_id=1, source_target_pairs={{2,4},{4,2},{10,12},{12,10},{18,20},{20,18},{26,28},{28,26},{3,5},... | collective-permute-start | bytes 2752520 | tf_op jit(solution)/shard_map/ppermute | solution.py:796
  18.0 0.0 collective-permute-done.2.refs_4_
  18.0 2.1 %collective-permute-done.3.far_ref.refs_5_ = f32[55,16,128]{2,1,0:T(8,128)S(1)} collective-permute-done((f32[55,16,128]{2,1,0:T(8,128)}, f32[55,16,128]{2,1,0:T(8,128)S(1)}, u32[]{:S(2)}, u32[]{:S(2)}) %collective-permute-start.3) | collective-permute-done | bytes 450592 | tf_op jit(solution)/shard_map/ppermute | solution.py:731
  20.1 0.7 collective-permute-start.4
  20.8 0.0 copy-start.5
  20.8 0.8 %copy-done.5 = f32[104,128]{1,0:T(8,128)S(1)} copy-done((f32[104,128]{1,0:T(8,128)S(1)}, f32[104,128]{1,0:T(8,128)}, u32[]{:S(2)}) %copy-start.5) | copy-done | bytes 53272
  21.6 1.0 %coast_tables.1 = (f32[9,32,128]{2,1,0:T(8,128)S(1)}, f32[8,32,128]{2,1,0:T(8,128)S(1)}, f32[4,144,8,128]{3,2,1,0:T(8,128)S(1)}, f32[8,8,128]{2,1,0:T(8,128)S(1)}) custom-call(s32[1]{0:T(128)} %bitcast.refs_0_.block_ref, f32[55,16,128]{2,1,0:T(8,128)S(1)} %collective-permute-done.3.far_ref.refs_5_, f32[104,128]{1,0:T(8,128)S(1)} %copy-done.5), custom_call_target="tpu_custom_call" | custom-call | flops 589824 | bytes 2359296 | tf_op jit(solution)/shard_map/coast_tables/pallas_call | solution.py:719
  22.6 0.0 copy-done.2
  22.6 0.0 copy-done.3
  22.6 0.0 copy-done.4
  22.6 0.0 copy-start
  22.6 0.0 copy-start.1
  22.7 3.4 %one_substep.2 = (f32[112,16,128]{2,1,0:T(8,128)S(1)}, f32[112,16,128]{2,1,0:T(8,128)S(1)}) custom-call(s32[1]{0:T(128)} %bitcast.refs_0_.block_ref, f32[55,16,128]{2,1,0:T(8,128)S(1)} %copy-done.2, f32[55,16,128]{2,1,0:T(8,128)S(1)} %copy-done.3, f32[36,16,128]{2,1,0:T(8,128)S(1)} %copy-done.4, f32[55,16,128]{2,1,0:T(8,128)S(1)} %collective-permute-done.2.refs_4_, ...), custom_call_target="tpu_custom_call" | custom-call | flops 23592960 | bytes 4718592 | tf_op jit(solution)/shard_map/one_substep/pallas_call | solution.py:759
  26.1 0.1 collective-permute-start.7
  26.1 3.6 %collective-permute-start.8 = (f32[112,16,128]{2,1,0:T(8,128)S(1)}, f32[112,16,128]{2,1,0:T(8,128)S(1)}, u32[]{:S(2)}, u32[]{:S(2)}) collective-permute-start(f32[112,16,128]{2,1,0:T(8,128)S(1)} %get-tuple-element.40.refs_2_), channel_id=1, source_target_pairs={{2,4},{4,2},{6,8},{8,6},{10,12},{12,10},{14,16},{16,14},{18,20},{2... | collective-permute-start | bytes 2752520 | tf_op jit(solution)/shard_map/ppermute | solution.py:731
  29.8 0.0 collective-permute-done.refs_3_
  29.8 19.8 %collective-permute-done.1.refs_4_ = f32[112,16,128]{2,1,0:T(8,128)S(1)} collective-permute-done((f32[112,16,128]{2,1,0:T(8,128)}, f32[112,16,128]{2,1,0:T(8,128)S(1)}, u32[]{:S(2)}, u32[]{:S(2)}) %collective-permute-start.1) | collective-permute-done | bytes 917536 | tf_op jit(solution)/shard_map/ppermute | solution.py:796
  49.6 0.0 collective-permute-done.4.refs_5_
  49.6 0.0 copy-done
  49.6 0.0 copy-done.1
  49.6 9.4 %two_substeps.2 = (f32[54,16,128]{2,1,0:T(8,128)S(1)}, f32[54,16,128]{2,1,0:T(8,128)S(1)}, f32[36,16,128]{2,1,0:T(8,128)S(1)}) custom-call(s32[1]{0:T(128)} %bitcast.refs_0_.block_ref, f32[112,16,128]{2,1,0:T(8,128)S(1)} %copy-done, f32[112,16,128]{2,1,0:T(8,128)S(1)} %copy-done.1, f32[112,16,128]{2,1,0:T(8,128)S(1)} %collective-permute-done.refs_3_, ...), custom_call_target="tpu_custom_call" | custom-call | flops 23592960 | bytes 4718592 | tf_op jit(solution)/shard_map/two_substeps/pallas_call | solution.py:759
  59.0 0.1 collective-permute-start.5
  59.1 3.7 %collective-permute-start.6 = (f32[54,16,128]{2,1,0:T(8,128)S(1)}, f32[54,16,128]{2,1,0:T(8,128)S(1)}, u32[]{:S(2)}, u32[]{:S(2)}) collective-permute-start(f32[54,16,128]{2,1,0:T(8,128)S(1)} %get-tuple-element.34.refs_2_), channel_id=1, source_target_pairs={{2,4},{4,2},{6,8},{8,6},{10,12},{12,10},{14,16},{16,14},{18,20},{2... | collective-permute-start | bytes 1327112 | tf_op jit(solution)/shard_map/ppermute | solution.py:731
  62.7 0.0 collective-permute-done.7.refs_3_
  62.7 0.0 collective-permute-done.8.refs_4_
  62.8 10.3 %two_substeps.3.refs_10_ = f32[1152,512]{1,0:T(8,128)} custom-call(s32[1]{0:T(128)} %bitcast.refs_0_.block_ref, f32[112,16,128]{2,1,0:T(8,128)S(1)} %get-tuple-element.39.refs_1_, f32[112,16,128]{2,1,0:T(8,128)S(1)} %get-tuple-element.40.refs_2_, f32[112,16,128]{2,1,0:T(8,128)S(1)} %collective-permute-done.7.refs_3_, ...), custom_call_target="tpu_custom_call" | custom-call | flops 23592960 | bytes 4718592 | tf_op jit(solution)/shard_map/two_substeps/pallas_call | solution.py:759
  73.1 0.0 collective-permute-done.5.refs_4_
  73.1 0.4 collective-permute-done.6.refs_5_
  73.5 3.8 %one_substep.3 = f32[1152,512]{1,0:T(8,128)} custom-call(s32[1]{0:T(128)} %bitcast.refs_0_.block_ref, f32[54,16,128]{2,1,0:T(8,128)S(1)} %get-tuple-element.33.refs_1_, f32[54,16,128]{2,1,0:T(8,128)S(1)} %get-tuple-element.34.refs_2_, f32[36,16,128]{2,1,0:T(8,128)S(1)} %get-tuple-element.35.refs_3_, ...), custom_call_target="tpu_custom_call", output_to_operand_aliasing={{}: (10, {})} | custom-call | flops 23592960 | bytes 4718592 | tf_op jit(solution)/shard_map/one_substep/pallas_call | solution.py:759
Async XLA Ops:
  4.4 13.6 %collective-permute-start.2 = (f32[55,16,128]{2,1,0:T(8,128)}, f32[55,16,128]{2,1,0:T(8,128)S(1)}, u32[]{:S(2)}, u32[]{:S(2)}) collective-permute-start(f32[55,16,128]{2,1,0:T(8,128)} %get-tuple-element.25.refs_1_), channel_id=1, source_target_pairs={{0,2},{2,0},{4,6},{6,4},{8,10},{10,8},{12,14},{14,12},{16,18},{18,... | collective-permute-start | bytes 1351688 | tf_op jit(solution)/shard_map/ppermute | solution.py:732
  4.5 15.6 %collective-permute-start.3 = (f32[55,16,128]{2,1,0:T(8,128)}, f32[55,16,128]{2,1,0:T(8,128)S(1)}, u32[]{:S(2)}, u32[]{:S(2)}) collective-permute-start(f32[55,16,128]{2,1,0:T(8,128)} %get-tuple-element.26.refs_2_), channel_id=1, source_target_pairs={{2,4},{4,2},{6,8},{8,6},{10,12},{12,10},{14,16},{16,14},{18,20},{2... | collective-permute-start | bytes 1351688 | tf_op jit(solution)/shard_map/ppermute | solution.py:731
  9.0 13.6 %copy-start.2 = (f32[55,16,128]{2,1,0:T(8,128)S(1)}, f32[55,16,128]{2,1,0:T(8,128)}, u32[]{:S(2)}) copy-start(f32[55,16,128]{2,1,0:T(8,128)} %get-tuple-element.25.refs_1_) | copy-start | bytes 1351684
  9.0 13.6 %copy-start.3 = (f32[55,16,128]{2,1,0:T(8,128)S(1)}, f32[55,16,128]{2,1,0:T(8,128)}, u32[]{:S(2)}) copy-start(f32[55,16,128]{2,1,0:T(8,128)} %get-tuple-element.26.refs_2_) | copy-start | bytes 1351684
  9.0 13.6 %copy-start.4 = (f32[36,16,128]{2,1,0:T(8,128)S(1)}, f32[36,16,128]{2,1,0:T(8,128)}, u32[]{:S(2)}) copy-start(f32[36,16,128]{2,1,0:T(8,128)} %get-tuple-element.36.refs_3_) | copy-start | bytes 884740
  14.4 15.4 %collective-permute-start = (f32[112,16,128]{2,1,0:T(8,128)}, f32[112,16,128]{2,1,0:T(8,128)S(1)}, u32[]{:S(2)}, u32[]{:S(2)}) collective-permute-start(f32[112,16,128]{2,1,0:T(8,128)} %get-tuple-element.23.refs_1_), channel_id=1, source_target_pairs={{0,2},{2,0},{4,6},{6,4},{8,10},{10,8},{12,14},{14,12},{16,18},{18,... | collective-permute-start | bytes 2752520 | tf_op jit(solution)/shard_map/ppermute | solution.py:796
  14.5 35.1 %collective-permute-start.1 = (f32[112,16,128]{2,1,0:T(8,128)}, f32[112,16,128]{2,1,0:T(8,128)S(1)}, u32[]{:S(2)}, u32[]{:S(2)}) collective-permute-start(f32[112,16,128]{2,1,0:T(8,128)} %get-tuple-element.27.refs_2_), channel_id=1, source_target_pairs={{2,4},{4,2},{10,12},{12,10},{18,20},{20,18},{26,28},{28,26},{3,5},... | collective-permute-start | bytes 2752520 | tf_op jit(solution)/shard_map/ppermute | solution.py:796
  20.1 29.5 %collective-permute-start.4 = (f32[112,16,128]{2,1,0:T(8,128)}, f32[112,16,128]{2,1,0:T(8,128)S(1)}, u32[]{:S(2)}, u32[]{:S(2)}) collective-permute-start(f32[112,16,128]{2,1,0:T(8,128)} %get-tuple-element.27.refs_2_), channel_id=1, source_target_pairs={{6,8},{8,6},{14,16},{16,14},{22,24},{24,22},{30,1},{1,30},{7,9},{9... | collective-permute-start | bytes 2752520 | tf_op jit(solution)/shard_map/ppermute | solution.py:798
  20.8 0.8 %copy-start.5 = (f32[104,128]{1,0:T(8,128)S(1)}, f32[104,128]{1,0:T(8,128)}, u32[]{:S(2)}) copy-start(f32[104,128]{1,0:T(8,128)} %get-tuple-element.28.kit_ref) | copy-start | bytes 159748
  22.6 27.0 %copy-start = (f32[112,16,128]{2,1,0:T(8,128)S(1)}, f32[112,16,128]{2,1,0:T(8,128)}, u32[]{:S(2)}) copy-start(f32[112,16,128]{2,1,0:T(8,128)} %get-tuple-element.23.refs_1_) | copy-start | bytes 2752516
  22.6 27.0 %copy-start.1 = (f32[112,16,128]{2,1,0:T(8,128)S(1)}, f32[112,16,128]{2,1,0:T(8,128)}, u32[]{:S(2)}) copy-start(f32[112,16,128]{2,1,0:T(8,128)} %get-tuple-element.27.refs_2_) | copy-start | bytes 2752516
  26.1 36.7 %collective-permute-start.7 = (f32[112,16,128]{2,1,0:T(8,128)S(1)}, f32[112,16,128]{2,1,0:T(8,128)S(1)}, u32[]{:S(2)}, u32[]{:S(2)}) collective-permute-start(f32[112,16,128]{2,1,0:T(8,128)S(1)} %get-tuple-element.39.refs_1_), channel_id=1, source_target_pairs={{0,2},{2,0},{4,6},{6,4},{8,10},{10,8},{12,14},{14,12},{16,18},{18,... | collective-permute-start | bytes 2752520 | tf_op jit(solution)/shard_map/ppermute | solution.py:732
  26.1 36.6 %collective-permute-start.8 = (f32[112,16,128]{2,1,0:T(8,128)S(1)}, f32[112,16,128]{2,1,0:T(8,128)S(1)}, u32[]{:S(2)}, u32[]{:S(2)}) collective-permute-start(f32[112,16,128]{2,1,0:T(8,128)S(1)} %get-tuple-element.40.refs_2_), channel_id=1, source_target_pairs={{2,4},{4,2},{6,8},{8,6},{10,12},{12,10},{14,16},{16,14},{18,20},{2... | collective-permute-start | bytes 2752520 | tf_op jit(solution)/shard_map/ppermute | solution.py:731
  59.0 14.1 %collective-permute-start.5 = (f32[54,16,128]{2,1,0:T(8,128)S(1)}, f32[54,16,128]{2,1,0:T(8,128)S(1)}, u32[]{:S(2)}, u32[]{:S(2)}) collective-permute-start(f32[54,16,128]{2,1,0:T(8,128)S(1)} %get-tuple-element.33.refs_1_), channel_id=1, source_target_pairs={{0,2},{2,0},{4,6},{6,4},{8,10},{10,8},{12,14},{14,12},{16,18},{18,... | collective-permute-start | bytes 1327112 | tf_op jit(solution)/shard_map/ppermute | solution.py:732
  59.1 14.4 %collective-permute-start.6 = (f32[54,16,128]{2,1,0:T(8,128)S(1)}, f32[54,16,128]{2,1,0:T(8,128)S(1)}, u32[]{:S(2)}, u32[]{:S(2)}) collective-permute-start(f32[54,16,128]{2,1,0:T(8,128)S(1)} %get-tuple-element.34.refs_2_), channel_id=1, source_target_pairs={{2,4},{4,2},{6,8},{8,6},{10,12},{12,10},{14,16},{16,14},{18,20},{2... | collective-permute-start | bytes 1327112 | tf_op jit(solution)/shard_map/ppermute | solution.py:731
